TPU v7x, 256 devices: a whole 4x4x8 slice. The times are simulated.
256 devices in a mesh: gx: 4 (over y), gy: 8 (over z), gz: 8 (over x, core).
Axes of the slice: x: 4, y: 4, z: 8, core: 2. Of those that a mesh axis runs over, the one named last changes fastest.
Arguments:
- populations: float32 [19, 16, 128, 1024], P(None, 'gx', 'gy', 'gz'), may hold values from 0 to 0.6, as said below
- design: float32 [16, 128, 1024], P('gx', 'gy', 'gz'), may hold values from 0 to 1
- labels: int32 [16, 128, 1024], P('gx', 'gy', 'gz'), may hold values from 1 to 4, as said below
Outputs:
- adjoint: float32 [19, 16, 128, 1024], P(None, 'gx', 'gy', 'gz')
- sensitivity: float32 [16, 128, 1024], P('gx', 'gy', 'gz')
- objective: float32 [], replicated
Inputs may be any that keep to these rules, and one draw needn't show every extreme that they name: `labels`: cells on the four side faces (x or y first or last) are 2; otherwise the first z layer is 3 and the last is 4; inside, cells are 1 or 2. Positive populations near equilibrium with density near 1 and speeds below 0.2.
All inputs are finite; a program needn't handle non-finite values.
Results may differ from a plain program's by a relative error of at most 0.0003.
Values sent between devices are 32-bit elements; how exact they have to be, the bound alone decides.
A program may use at most 64 MiB of HBM per device.

v0:
```python
import jax
import jax.numpy as jnp
from jax import lax
from jax.sharding import PartitionSpec as P

VELOCITY = [
    (0, 0, 0),
    (1, 0, 0),
    (-1, 0, 0),
    (0, 1, 0),
    (0, -1, 0),
    (0, 0, 1),
    (0, 0, -1),
    (1, 1, 0),
    (-1, -1, 0),
    (1, -1, 0),
    (-1, 1, 0),
    (1, 0, 1),
    (-1, 0, -1),
    (1, 0, -1),
    (-1, 0, 1),
    (0, 1, 1),
    (0, -1, -1),
    (0, 1, -1),
    (0, -1, 1),
]
WEIGHTS = [1.0 / 3.0] + [1.0 / 18.0] * 6 + [1.0 / 36.0] * 12
OPPOSITE = [0, 2, 1, 4, 3, 6, 5, 8, 7, 10, 9, 12, 11, 14, 13, 16, 15, 18, 17]
RELAX = 1.6
INFLOW = 0.05


def padded_2(cells, sides, width):
    for axis, dim in sides:
        count = lax.axis_size(axis)
        ends = count - 1
        head = lax.slice_in_dim(cells, 0, width, axis=dim)
        tail = lax.slice_in_dim(cells, cells.shape[dim] - width, cells.shape[dim], axis=dim)
        cells = jnp.concatenate(
            [
                lax.ppermute(tail, axis, [(i, (i + 1) % count) for i in range(ends)]),
                cells,
                lax.ppermute(head, axis, [((i + 1) % count, i) for i in range(ends)]),
            ],
            axis=dim,
        )
    return cells


def equilibrium(density, speed):
    square = speed[0] * speed[0] + speed[1] * speed[1] + speed[2] * speed[2]
    rows = []
    for index in range(19):
        along = (
            VELOCITY[index][0] * speed[0]
            + VELOCITY[index][1] * speed[1]
            + VELOCITY[index][2] * speed[2]
        )
        rows.append(
            WEIGHTS[index] * density * (1.0 + 3.0 * along + 4.5 * along * along - 1.5 * square)
        )
    return jnp.stack(rows)


def velocity(field, safe):
    result = []
    for axis in range(3):
        total = jnp.zeros_like(safe)
        for index in range(19):
            if VELOCITY[index][axis] != 0:
                total = total + VELOCITY[index][axis] * field[index]
        result.append(total / safe)
    return result


def collide(field, design, labels):
    density = jnp.sum(field, axis=0)
    safe = jnp.where(labels > 0, density, 1.0)
    speed = velocity(field, safe)
    damping = 1.0 / (1.0 + design)
    relaxed = field - RELAX * (field - equilibrium(safe, [s * damping for s in speed]))
    bounce = jnp.stack([field[j] for j in OPPOSITE])
    ones = jnp.ones_like(density)
    zeros = jnp.zeros_like(density)
    inlet = equilibrium(ones, [zeros, zeros, zeros + INFLOW])
    outlet = equilibrium(ones, speed)
    marks = labels[None]
    result = jnp.where(marks == 1, relaxed, 0.0)
    result = jnp.where(marks == 2, bounce, result)
    result = jnp.where(marks == 3, inlet, result)
    return jnp.where(marks == 4, outlet, result)


def dissipation(field, design, labels):
    density = jnp.sum(field, axis=0)
    safe = jnp.where(labels > 0, density, 1.0)
    speed = velocity(field, safe)
    square = speed[0] * speed[0] + speed[1] * speed[1] + speed[2] * speed[2]
    return 10.0 * jnp.sum(jnp.where(labels == 1, design * safe * square, 0.0))


def stream(field, sign):
    padded = padded_2(field, (("gx", 1), ("gy", 2), ("gz", 3)), 1)
    sizes = field.shape[1:]
    rows = []
    for index in range(19):
        start = [1 - sign * VELOCITY[index][a] for a in range(3)]
        rows.append(
            padded[
                index,
                start[0] : start[0] + sizes[0],
                start[1] : start[1] + sizes[1],
                start[2] : start[2] + sizes[2],
            ]
        )
    return jnp.stack(rows)


def body(populations, design, labels):
    middle = stream(collide(populations, design, labels), 1)
    second = stream(collide(middle, design, labels), 1)
    local_total, (final_grad, direct) = jax.value_and_grad(dissipation, argnums=(0, 1))(
        second, design, labels
    )
    _, back_two = jax.vjp(lambda f, d: collide(f, d, labels), middle, design)
    back_mid, sens_two = back_two(stream(final_grad, -1))
    _, back_one = jax.vjp(lambda f, d: collide(f, d, labels), populations, design)
    adjoint, sens_one = back_one(stream(back_mid, -1))
    raw = direct + sens_two + sens_one
    totals = lax.psum((local_total, jnp.sum(jnp.abs(raw))), ("gx", "gy", "gz"))
    cells = (
        design.shape[0]
        * design.shape[1]
        * design.shape[2]
        * lax.axis_size("gx")
        * lax.axis_size("gy")
        * lax.axis_size("gz")
    )
    scale = totals[1] / cells + 1e-06
    return (adjoint, raw / scale, 20.0 * totals[0] / cells)


def solution(mesh):
    in_specs = (P(None, "gx", "gy", "gz"), P("gx", "gy", "gz"), P("gx", "gy", "gz"))
    out_specs = (P(None, "gx", "gy", "gz"), P("gx", "gy", "gz"), P())
    return jax.shard_map(body, mesh=mesh, in_specs=in_specs, out_specs=out_specs, check_vma=False)
```

profile of v0, /device:TPU:1, one launch (start us, length us, event | category | flops | bytes accessed | tf_op | source)
XLA Modules:
  0.0 297.0 jit_solution(9096316135089324598)
XLA Ops:
  17.3 4.0 %collective-permute-start = (f32[19,1,16,128]{3,2,1,0:T(8,128)S(1)}, f32[19,1,16,128]{3,2,1,0:T(8,128)S(1)}, u32[]{:S(2)}, u32[]{:S(2)}) collective-permute-start(f32[19,1,16,128]{3,2,1,0:T(8,128)S(1)} %get-tuple-element.363), channel_id=1, source_target_pairs={{0,64},{64,128},{128,192},{1,65},{65,129},{129,193},{2,66},{66,130... | collective-permute-start | bytes 466952 | tf_op jit(solution)/shard_map/ppermute | solution.py:41
  24.0 3.8 %collective-permute-done.1 = f32[19,1,16,128]{3,2,1,0:T(8,128)S(1)} collective-permute-done((f32[19,1,16,128]{3,2,1,0:T(8,128)S(1)}, f32[19,1,16,128]{3,2,1,0:T(8,128)S(1)}, u32[]{:S(2)}, u32[]{:S(2)}) %collective-permute-start.1) | collective-permute-done | bytes 155680 | tf_op jit(solution)/shard_map/ppermute | solution.py:43
  27.9 3.5 %collective-permute-start.2 = (f32[19,6,1,128]{3,2,1,0:T(1,128)S(1)}, f32[19,6,1,128]{3,2,1,0:T(1,128)S(1)}, u32[]{:S(2)}, u32[]{:S(2)}) collective-permute-start(f32[19,6,1,128]{3,2,1,0:T(1,128)S(1)} %get-tuple-element.221), channel_id=1, source_target_pairs={{0,8},{8,16},{16,24},{24,32},{32,40},{40,48},{48,56},{1,9},{9,17},... | collective-permute-start | bytes 175112 | tf_op jit(solution)/shard_map/ppermute | solution.py:41
  32.8 3.8 %collective-permute-done.3 = f32[19,6,1,128]{3,2,1,0:T(1,128)S(1)} collective-permute-done((f32[19,6,1,128]{3,2,1,0:T(1,128)S(1)}, f32[19,6,1,128]{3,2,1,0:T(1,128)S(1)}, u32[]{:S(2)}, u32[]{:S(2)}) %collective-permute-start.3) | collective-permute-done | bytes 58400 | tf_op jit(solution)/shard_map/ppermute | solution.py:43
  38.4 2.1 copy.62
  40.4 6.1 %collective-permute-start.4 = (f32[19,6,18,1]{0,3,2,1:T(1,128)S(1)}, f32[19,6,18,1]{0,3,2,1:T(1,128)S(1)}, u32[]{:S(2)}, u32[]{:S(2)}) collective-permute-start(f32[19,6,18,1]{0,3,2,1:T(1,128)S(1)} %copy.62), channel_id=1, source_target_pairs={{0,1},{1,2},{2,3},{3,4},{4,5},{5,6},{6,7},{8,9},{9,10},{10,11},{11... | collective-permute-start | bytes 24632 | tf_op jit(solution)/shard_map/ppermute | solution.py:41
  52.8 2.1 copy.65
  69.1 3.2 %collective-permute-start.6 = (f32[19,1,16,128]{3,2,1,0:T(8,128)S(1)}, f32[19,1,16,128]{3,2,1,0:T(8,128)S(1)}, u32[]{:S(2)}, u32[]{:S(2)}) collective-permute-start(f32[19,1,16,128]{3,2,1,0:T(8,128)S(1)} %get-tuple-element.360), channel_id=1, source_target_pairs={{0,64},{64,128},{128,192},{1,65},{65,129},{129,193},{2,66},{66,130... | collective-permute-start | bytes 466952 | tf_op jit(solution)/shard_map/ppermute | solution.py:41
  74.4 3.9 %collective-permute-done.7 = f32[19,1,16,128]{3,2,1,0:T(8,128)S(1)} collective-permute-done((f32[19,1,16,128]{3,2,1,0:T(8,128)S(1)}, f32[19,1,16,128]{3,2,1,0:T(8,128)S(1)}, u32[]{:S(2)}, u32[]{:S(2)}) %collective-permute-start.7) | collective-permute-done | bytes 155680 | tf_op jit(solution)/shard_map/ppermute | solution.py:43
  78.4 3.5 %collective-permute-start.8 = (f32[19,6,1,128]{3,2,1,0:T(1,128)S(1)}, f32[19,6,1,128]{3,2,1,0:T(1,128)S(1)}, u32[]{:S(2)}, u32[]{:S(2)}) collective-permute-start(f32[19,6,1,128]{3,2,1,0:T(1,128)S(1)} %get-tuple-element.218), channel_id=1, source_target_pairs={{0,8},{8,16},{16,24},{24,32},{32,40},{40,48},{48,56},{1,9},{9,17},... | collective-permute-start | bytes 175112 | tf_op jit(solution)/shard_map/ppermute | solution.py:41
  83.3 5.0 %collective-permute-done.9 = f32[19,6,1,128]{3,2,1,0:T(1,128)S(1)} collective-permute-done((f32[19,6,1,128]{3,2,1,0:T(1,128)S(1)}, f32[19,6,1,128]{3,2,1,0:T(1,128)S(1)}, u32[]{:S(2)}, u32[]{:S(2)}) %collective-permute-start.9) | collective-permute-done | bytes 58400 | tf_op jit(solution)/shard_map/ppermute | solution.py:43
  90.1 2.7 copy.66
  92.8 6.3 %collective-permute-start.10 = (f32[19,6,18,1]{0,3,2,1:T(1,128)}, f32[19,6,18,1]{0,3,2,1:T(1,128)}, u32[]{:S(2)}, u32[]{:S(2)}) collective-permute-start(f32[19,6,18,1]{0,3,2,1:T(1,128)} %copy.66), channel_id=1, source_target_pairs={{0,1},{1,2},{2,3},{3,4},{4,5},{5,6},{6,7},{8,9},{9,10},{10,11},{11... | collective-permute-start | bytes 24632 | tf_op jit(solution)/shard_map/ppermute | solution.py:41
  103.1 3.2 %collective-permute-done.11 = f32[19,6,18,1]{0,3,2,1:T(1,128)} collective-permute-done((f32[19,6,18,1]{0,3,2,1:T(1,128)}, f32[19,6,18,1]{0,3,2,1:T(1,128)}, u32[]{:S(2)}, u32[]{:S(2)}) %collective-permute-start.11) | collective-permute-done | bytes 8240 | tf_op jit(solution)/shard_map/ppermute | solution.py:43
  115.2 4.0 %collective-permute-start.13 = (f32[19,1,16,128]{3,2,1,0:T(8,128)S(1)}, f32[19,1,16,128]{3,2,1,0:T(8,128)S(1)}, u32[]{:S(2)}, u32[]{:S(2)}) collective-permute-start(f32[19,1,16,128]{3,2,1,0:T(8,128)S(1)} %get-tuple-element.358), channel_id=1, source_target_pairs={{0,64},{64,128},{128,192},{1,65},{65,129},{129,193},{2,66},{66,130... | collective-permute-start | bytes 466952 | tf_op jit(solution)/shard_map/ppermute | solution.py:41
  122.8 5.7 %collective-permute-start.15 = (f32[19,6,1,128]{3,2,1,0:T(1,128)S(1)}, f32[19,6,1,128]{3,2,1,0:T(1,128)S(1)}, u32[]{:S(2)}, u32[]{:S(2)}) collective-permute-start(f32[19,6,1,128]{3,2,1,0:T(1,128)S(1)} %get-tuple-element.214), channel_id=1, source_target_pairs={{0,8},{8,16},{16,24},{24,32},{32,40},{40,48},{48,56},{1,9},{9,17},... | collective-permute-start | bytes 175112 | tf_op jit(solution)/shard_map/ppermute | solution.py:41
  131.5 2.7 copy.70
  137.5 5.1 %collective-permute-start.17 = (f32[19,6,18,1]{0,3,2,1:T(1,128)}, f32[19,6,18,1]{0,3,2,1:T(1,128)}, u32[]{:S(2)}, u32[]{:S(2)}) collective-permute-start(f32[19,6,18,1]{0,3,2,1:T(1,128)} %copy.72), channel_id=1, source_target_pairs={{0,1},{1,2},{2,3},{3,4},{4,5},{5,6},{6,7},{8,9},{9,10},{10,11},{11... | collective-permute-start | bytes 24632 | tf_op jit(solution)/shard_map/ppermute | solution.py:41
  145.8 3.0 copy.73
  164.2 4.7 %collective-permute-start.19 = (f32[19,1,16,128]{3,2,1,0:T(8,128)S(1)}, f32[19,1,16,128]{3,2,1,0:T(8,128)S(1)}, u32[]{:S(2)}, u32[]{:S(2)}) collective-permute-start(f32[19,1,16,128]{3,2,1,0:T(8,128)S(1)} %get-tuple-element.338), channel_id=1, source_target_pairs={{0,64},{64,128},{128,192},{1,65},{65,129},{129,193},{2,66},{66,130... | collective-permute-start | bytes 466952 | tf_op jit(solution)/shard_map/ppermute | solution.py:41
  172.4 4.6 %collective-permute-start.21 = (f32[19,6,1,128]{3,2,1,0:T(1,128)S(1)}, f32[19,6,1,128]{3,2,1,0:T(1,128)S(1)}, u32[]{:S(2)}, u32[]{:S(2)}) collective-permute-start(f32[19,6,1,128]{3,2,1,0:T(1,128)S(1)} %get-tuple-element.212), channel_id=1, source_target_pairs={{0,8},{8,16},{16,24},{24,32},{32,40},{40,48},{48,56},{1,9},{9,17},... | collective-permute-start | bytes 175112 | tf_op jit(solution)/shard_map/ppermute | solution.py:41
  184.8 5.2 %collective-permute-start.23 = (f32[19,6,18,1]{0,3,2,1:T(1,128)S(1)}, f32[19,6,18,1]{0,3,2,1:T(1,128)S(1)}, u32[]{:S(2)}, u32[]{:S(2)}) collective-permute-start(f32[19,6,18,1]{0,3,2,1:T(1,128)S(1)} %copy.76), channel_id=1, source_target_pairs={{0,1},{1,2},{2,3},{3,4},{4,5},{5,6},{6,7},{8,9},{9,10},{10,11},{11... | collective-permute-start | bytes 24632 | tf_op jit(solution)/shard_map/ppermute | solution.py:41
  192.3 2.2 copy.77
  209.6 80.5 %all-reduce.126 = (f32[]{:T(128)}, f32[]{:T(128)}) all-reduce(f32[]{:T(128)} %get-tuple-element.11, f32[]{:T(128)S(6)} %mul.5432), channel_id=1, replica_groups=mesh['gx'=4,'gy'=8,'gz'=8] {'gx','gy','gz'}, use_global_device_ids=true, to_apply=%region_2.3 | all-reduce | flops 2 | bytes 16 | tf_op jit(solution)/shard_map/psum | solution.py:130
  (445 shorter events, 120.2 us)
Async XLA Ops:
  17.3 6.7 %collective-permute-start = (f32[19,1,16,128]{3,2,1,0:T(8,128)S(1)}, f32[19,1,16,128]{3,2,1,0:T(8,128)S(1)}, u32[]{:S(2)}, u32[]{:S(2)}) collective-permute-start(f32[19,1,16,128]{3,2,1,0:T(8,128)S(1)} %get-tuple-element.363), channel_id=1, source_target_pairs={{0,64},{64,128},{128,192},{1,65},{65,129},{129,193},{2,66},{66,130... | collective-permute-start | bytes 466952 | tf_op jit(solution)/shard_map/ppermute | solution.py:41
  21.3 6.5 %collective-permute-start.1 = (f32[19,1,16,128]{3,2,1,0:T(8,128)S(1)}, f32[19,1,16,128]{3,2,1,0:T(8,128)S(1)}, u32[]{:S(2)}, u32[]{:S(2)}) collective-permute-start(f32[19,1,16,128]{3,2,1,0:T(8,128)S(1)} %get-tuple-element.362), channel_id=1, source_target_pairs={{64,0},{128,64},{192,128},{65,1},{129,65},{193,129},{66,2},{130,66... | collective-permute-start | bytes 466952 | tf_op jit(solution)/shard_map/ppermute | solution.py:43
  27.9 4.9 %collective-permute-start.2 = (f32[19,6,1,128]{3,2,1,0:T(1,128)S(1)}, f32[19,6,1,128]{3,2,1,0:T(1,128)S(1)}, u32[]{:S(2)}, u32[]{:S(2)}) collective-permute-start(f32[19,6,1,128]{3,2,1,0:T(1,128)S(1)} %get-tuple-element.221), channel_id=1, source_target_pairs={{0,8},{8,16},{16,24},{24,32},{32,40},{40,48},{48,56},{1,9},{9,17},... | collective-permute-start | bytes 175112 | tf_op jit(solution)/shard_map/ppermute | solution.py:41
  31.5 5.1 %collective-permute-start.3 = (f32[19,6,1,128]{3,2,1,0:T(1,128)S(1)}, f32[19,6,1,128]{3,2,1,0:T(1,128)S(1)}, u32[]{:S(2)}, u32[]{:S(2)}) collective-permute-start(f32[19,6,1,128]{3,2,1,0:T(1,128)S(1)} %get-tuple-element.220), channel_id=1, source_target_pairs={{8,0},{16,8},{24,16},{32,24},{40,32},{48,40},{56,48},{9,1},{17,9},... | collective-permute-start | bytes 175112 | tf_op jit(solution)/shard_map/ppermute | solution.py:43
  40.4 9.9 %collective-permute-start.4 = (f32[19,6,18,1]{0,3,2,1:T(1,128)S(1)}, f32[19,6,18,1]{0,3,2,1:T(1,128)S(1)}, u32[]{:S(2)}, u32[]{:S(2)}) collective-permute-start(f32[19,6,18,1]{0,3,2,1:T(1,128)S(1)} %copy.62), channel_id=1, source_target_pairs={{0,1},{1,2},{2,3},{3,4},{4,5},{5,6},{6,7},{8,9},{9,10},{10,11},{11... | collective-permute-start | bytes 24632 | tf_op jit(solution)/shard_map/ppermute | solution.py:41
  47.3 5.5 %collective-permute-start.5 = (f32[19,6,18,1]{0,3,2,1:T(1,128)S(1)}, f32[19,6,18,1]{0,3,2,1:T(1,128)S(1)}, u32[]{:S(2)}, u32[]{:S(2)}) collective-permute-start(f32[19,6,18,1]{0,3,2,1:T(1,128)S(1)} %copy.64), channel_id=1, source_target_pairs={{1,0},{2,1},{3,2},{4,3},{5,4},{6,5},{7,6},{9,8},{10,9},{11,10},{12... | collective-permute-start | bytes 24632 | tf_op jit(solution)/shard_map/ppermute | solution.py:43
  69.1 5.4 %collective-permute-start.6 = (f32[19,1,16,128]{3,2,1,0:T(8,128)S(1)}, f32[19,1,16,128]{3,2,1,0:T(8,128)S(1)}, u32[]{:S(2)}, u32[]{:S(2)}) collective-permute-start(f32[19,1,16,128]{3,2,1,0:T(8,128)S(1)} %get-tuple-element.360), channel_id=1, source_target_pairs={{0,64},{64,128},{128,192},{1,65},{65,129},{129,193},{2,66},{66,130... | collective-permute-start | bytes 466952 | tf_op jit(solution)/shard_map/ppermute | solution.py:41
  72.3 6.1 %collective-permute-start.7 = (f32[19,1,16,128]{3,2,1,0:T(8,128)S(1)}, f32[19,1,16,128]{3,2,1,0:T(8,128)S(1)}, u32[]{:S(2)}, u32[]{:S(2)}) collective-permute-start(f32[19,1,16,128]{3,2,1,0:T(8,128)S(1)} %get-tuple-element.361), channel_id=1, source_target_pairs={{64,0},{128,64},{192,128},{65,1},{129,65},{193,129},{66,2},{130,66... | collective-permute-start | bytes 466952 | tf_op jit(solution)/shard_map/ppermute | solution.py:43
  78.4 4.9 %collective-permute-start.8 = (f32[19,6,1,128]{3,2,1,0:T(1,128)S(1)}, f32[19,6,1,128]{3,2,1,0:T(1,128)S(1)}, u32[]{:S(2)}, u32[]{:S(2)}) collective-permute-start(f32[19,6,1,128]{3,2,1,0:T(1,128)S(1)} %get-tuple-element.218), channel_id=1, source_target_pairs={{0,8},{8,16},{16,24},{24,32},{32,40},{40,48},{48,56},{1,9},{9,17},... | collective-permute-start | bytes 175112 | tf_op jit(solution)/shard_map/ppermute | solution.py:41
  82.0 6.3 %collective-permute-start.9 = (f32[19,6,1,128]{3,2,1,0:T(1,128)S(1)}, f32[19,6,1,128]{3,2,1,0:T(1,128)S(1)}, u32[]{:S(2)}, u32[]{:S(2)}) collective-permute-start(f32[19,6,1,128]{3,2,1,0:T(1,128)S(1)} %get-tuple-element.219), channel_id=1, source_target_pairs={{8,0},{16,8},{24,16},{32,24},{40,32},{48,40},{56,48},{9,1},{17,9},... | collective-permute-start | bytes 175112 | tf_op jit(solution)/shard_map/ppermute | solution.py:43
  92.8 16.8 %collective-permute-start.10 = (f32[19,6,18,1]{0,3,2,1:T(1,128)}, f32[19,6,18,1]{0,3,2,1:T(1,128)}, u32[]{:S(2)}, u32[]{:S(2)}) collective-permute-start(f32[19,6,18,1]{0,3,2,1:T(1,128)} %copy.66), channel_id=1, source_target_pairs={{0,1},{1,2},{2,3},{3,4},{4,5},{5,6},{6,7},{8,9},{9,10},{10,11},{11... | collective-permute-start | bytes 24632 | tf_op jit(solution)/shard_map/ppermute | solution.py:41
  100.5 5.8 %collective-permute-start.11 = (f32[19,6,18,1]{0,3,2,1:T(1,128)}, f32[19,6,18,1]{0,3,2,1:T(1,128)}, u32[]{:S(2)}, u32[]{:S(2)}) collective-permute-start(f32[19,6,18,1]{0,3,2,1:T(1,128)} %copy.68), channel_id=1, source_target_pairs={{1,0},{2,1},{3,2},{4,3},{5,4},{6,5},{7,6},{9,8},{10,9},{11,10},{12... | collective-permute-start | bytes 24632 | tf_op jit(solution)/shard_map/ppermute | solution.py:43
  113.9 6.6 %collective-permute-start.12 = (f32[19,1,16,128]{3,2,1,0:T(8,128)S(1)}, f32[19,1,16,128]{3,2,1,0:T(8,128)S(1)}, u32[]{:S(2)}, u32[]{:S(2)}) collective-permute-start(f32[19,1,16,128]{3,2,1,0:T(8,128)S(1)} %get-tuple-element.359), channel_id=1, source_target_pairs={{64,0},{128,64},{192,128},{65,1},{129,65},{193,129},{66,2},{130,66... | collective-permute-start | bytes 466952 | tf_op jit(solution)/shard_map/ppermute | solution.py:43
  115.2 6.3 %collective-permute-start.13 = (f32[19,1,16,128]{3,2,1,0:T(8,128)S(1)}, f32[19,1,16,128]{3,2,1,0:T(8,128)S(1)}, u32[]{:S(2)}, u32[]{:S(2)}) collective-permute-start(f32[19,1,16,128]{3,2,1,0:T(8,128)S(1)} %get-tuple-element.358), channel_id=1, source_target_pairs={{0,64},{64,128},{128,192},{1,65},{65,129},{129,193},{2,66},{66,130... | collective-permute-start | bytes 466952 | tf_op jit(solution)/shard_map/ppermute | solution.py:41
  121.5 8.2 %collective-permute-start.14 = (f32[19,6,1,128]{3,2,1,0:T(1,128)S(1)}, f32[19,6,1,128]{3,2,1,0:T(1,128)S(1)}, u32[]{:S(2)}, u32[]{:S(2)}) collective-permute-start(f32[19,6,1,128]{3,2,1,0:T(1,128)S(1)} %get-tuple-element.215), channel_id=1, source_target_pairs={{8,0},{16,8},{24,16},{32,24},{40,32},{48,40},{56,48},{9,1},{17,9},... | collective-permute-start | bytes 175112 | tf_op jit(solution)/shard_map/ppermute | solution.py:43
  122.8 6.9 %collective-permute-start.15 = (f32[19,6,1,128]{3,2,1,0:T(1,128)S(1)}, f32[19,6,1,128]{3,2,1,0:T(1,128)S(1)}, u32[]{:S(2)}, u32[]{:S(2)}) collective-permute-start(f32[19,6,1,128]{3,2,1,0:T(1,128)S(1)} %get-tuple-element.214), channel_id=1, source_target_pairs={{0,8},{8,16},{16,24},{24,32},{32,40},{40,48},{48,56},{1,9},{9,17},... | collective-permute-start | bytes 175112 | tf_op jit(solution)/shard_map/ppermute | solution.py:41
  134.2 9.7 %collective-permute-start.16 = (f32[19,6,18,1]{0,3,2,1:T(1,128)}, f32[19,6,18,1]{0,3,2,1:T(1,128)}, u32[]{:S(2)}, u32[]{:S(2)}) collective-permute-start(f32[19,6,18,1]{0,3,2,1:T(1,128)} %copy.70), channel_id=1, source_target_pairs={{1,0},{2,1},{3,2},{4,3},{5,4},{6,5},{7,6},{9,8},{10,9},{11,10},{12... | collective-permute-start | bytes 24632 | tf_op jit(solution)/shard_map/ppermute | solution.py:43
  137.5 8.3 %collective-permute-start.17 = (f32[19,6,18,1]{0,3,2,1:T(1,128)}, f32[19,6,18,1]{0,3,2,1:T(1,128)}, u32[]{:S(2)}, u32[]{:S(2)}) collective-permute-start(f32[19,6,18,1]{0,3,2,1:T(1,128)} %copy.72), channel_id=1, source_target_pairs={{0,1},{1,2},{2,3},{3,4},{4,5},{5,6},{6,7},{8,9},{9,10},{10,11},{11... | collective-permute-start | bytes 24632 | tf_op jit(solution)/shard_map/ppermute | solution.py:41
  162.9 6.7 %collective-permute-start.18 = (f32[19,1,16,128]{3,2,1,0:T(8,128)S(1)}, f32[19,1,16,128]{3,2,1,0:T(8,128)S(1)}, u32[]{:S(2)}, u32[]{:S(2)}) collective-permute-start(f32[19,1,16,128]{3,2,1,0:T(8,128)S(1)} %get-tuple-element.339), channel_id=1, source_target_pairs={{64,0},{128,64},{192,128},{65,1},{129,65},{193,129},{66,2},{130,66... | collective-permute-start | bytes 466952 | tf_op jit(solution)/shard_map/ppermute | solution.py:43
  164.2 6.9 %collective-permute-start.19 = (f32[19,1,16,128]{3,2,1,0:T(8,128)S(1)}, f32[19,1,16,128]{3,2,1,0:T(8,128)S(1)}, u32[]{:S(2)}, u32[]{:S(2)}) collective-permute-start(f32[19,1,16,128]{3,2,1,0:T(8,128)S(1)} %get-tuple-element.338), channel_id=1, source_target_pairs={{0,64},{64,128},{128,192},{1,65},{65,129},{129,193},{2,66},{66,130... | collective-permute-start | bytes 466952 | tf_op jit(solution)/shard_map/ppermute | solution.py:41
  171.1 7.2 %collective-permute-start.20 = (f32[19,6,1,128]{3,2,1,0:T(1,128)S(1)}, f32[19,6,1,128]{3,2,1,0:T(1,128)S(1)}, u32[]{:S(2)}, u32[]{:S(2)}) collective-permute-start(f32[19,6,1,128]{3,2,1,0:T(1,128)S(1)} %get-tuple-element.213), channel_id=1, source_target_pairs={{8,0},{16,8},{24,16},{32,24},{40,32},{48,40},{56,48},{9,1},{17,9},... | collective-permute-start | bytes 175112 | tf_op jit(solution)/shard_map/ppermute | solution.py:43
  172.4 5.9 %collective-permute-start.21 = (f32[19,6,1,128]{3,2,1,0:T(1,128)S(1)}, f32[19,6,1,128]{3,2,1,0:T(1,128)S(1)}, u32[]{:S(2)}, u32[]{:S(2)}) collective-permute-start(f32[19,6,1,128]{3,2,1,0:T(1,128)S(1)} %get-tuple-element.212), channel_id=1, source_target_pairs={{0,8},{8,16},{16,24},{24,32},{32,40},{40,48},{48,56},{1,9},{9,17},... | collective-permute-start | bytes 175112 | tf_op jit(solution)/shard_map/ppermute | solution.py:41
  182.2 9.1 %collective-permute-start.22 = (f32[19,6,18,1]{0,3,2,1:T(1,128)S(1)}, f32[19,6,18,1]{0,3,2,1:T(1,128)S(1)}, u32[]{:S(2)}, u32[]{:S(2)}) collective-permute-start(f32[19,6,18,1]{0,3,2,1:T(1,128)S(1)} %copy.74), channel_id=1, source_target_pairs={{1,0},{2,1},{3,2},{4,3},{5,4},{6,5},{7,6},{9,8},{10,9},{11,10},{12... | collective-permute-start | bytes 24632 | tf_op jit(solution)/shard_map/ppermute | solution.py:43
  184.8 7.5 %collective-permute-start.23 = (f32[19,6,18,1]{0,3,2,1:T(1,128)S(1)}, f32[19,6,18,1]{0,3,2,1:T(1,128)S(1)}, u32[]{:S(2)}, u32[]{:S(2)}) collective-permute-start(f32[19,6,18,1]{0,3,2,1:T(1,128)S(1)} %copy.76), channel_id=1, source_target_pairs={{0,1},{1,2},{2,3},{3,4},{4,5},{5,6},{6,7},{8,9},{9,10},{10,11},{11... | collective-permute-start | bytes 24632 | tf_op jit(solution)/shard_map/ppermute | solution.py:41
  (94 other events, 815.8 us)
where the time goes:
time: 299 us; the launch traced here: 297 us
  blocking collectives  80.5 us (27%)
  starting transfers between devices  74 us (25%)
  other arithmetic  67.4 us (23%)
  local copies, waits for them, and re-layouts  43.4 us (15%)
  waiting for transfers between devices  25.9 us (9%)
  between operations  5.88 us (2%)
    psum x1, blocking collectives, body(): totals = lax.psum((local_total, jnp.sum(jnp.abs(raw))), ('gx', 'gy', 'gz'))  80.5 us
    ppermute x12, starting transfers between devices, padded_2(): lax.ppermute(tail, axis, [(i, (i + 1) % count) for i in range(ends)])  56 us
    unnamed x106, other arithmetic  46.5 us
    ppermute x12, waiting for transfers between devices, padded_2(): lax.ppermute(head, axis, [((i + 1) % count, i) for i in range(ends)])  21.2 us
    ppermute x12, starting transfers between devices, padded_2(): lax.ppermute(head, axis, [((i + 1) % count, i) for i in range(ends)])  18 us
    slice x10, local copies, waits for them, and re-layouts, padded_2(): lax.slice_in_dim(cells, cells.shape[dim] - width, cells.shape[dim], axis=...  11.6 us
    slice x6, local copies, waits for them, and re-layouts, padded_2(): head = lax.slice_in_dim(cells, 0, width, axis=dim)  8.44 us
    ppermute x4, local copies, waits for them, and re-layouts, padded_2(): lax.ppermute(tail, axis, [(i, (i + 1) % count) for i in range(ends)])  8.03 us
  transfers between devices with their start and end apart: 24, of which 11 were waited for; matrix products, arithmetic and copies ran while one was open for 7% of the time, Pallas kernels for 0%

commit v1 on v0

v1 whole, which is shorter than its diff:
```python
import jax
import jax.numpy as jnp
from jax import lax
from jax.experimental import pallas as pl
from jax.experimental.pallas import tpu as pltpu
from jax.sharding import PartitionSpec as P

VELOCITY = [
    (0, 0, 0),
    (1, 0, 0),
    (-1, 0, 0),
    (0, 1, 0),
    (0, -1, 0),
    (0, 0, 1),
    (0, 0, -1),
    (1, 1, 0),
    (-1, -1, 0),
    (1, -1, 0),
    (-1, 1, 0),
    (1, 0, 1),
    (-1, 0, -1),
    (1, 0, -1),
    (-1, 0, 1),
    (0, 1, 1),
    (0, -1, -1),
    (0, 1, -1),
    (0, -1, 1),
]
OPPOSITE = [0, 2, 1, 4, 3, 6, 5, 8, 7, 10, 9, 12, 11, 14, 13, 16, 15, 18, 17]
PAIRS = [1, 3, 5, 7, 9, 11, 13, 15, 17]
RELAX = 1.6
INFLOW = 0.05
MESH = pl.DeviceIdType.MESH
F32 = jnp.float32

ORDER = [9, 1, 11, 13, 7, 3, 15, 17, 10, 2, 12, 14, 8, 4, 16, 18, 9, 5, 6, 0]
SLOT = {index: ORDER.index(index) for index in range(19)}
TWIN = 16
ZPLUS = [5, 11, 14, 15, 18]
ZMINUS = [6, 12, 13, 16, 17]
ROW = 8

NX, NY, NZ = 4, 16, 128
HALVES = NY // 8
ROUNDS = 4


def neighbours():
    found = []
    for dx, dy, dz in VELOCITY[1:]:
        found.append((dx, dy, dz))
    return found


NEIGHBOURS = neighbours()


def kernel(
    sizes,
    pop_hbm,
    design_hbm,
    labels_hbm,
    adj_hbm,
    sens_ref,
    obj_ref,
    pop,
    design,
    labels,
    adj,
    pads,
    zsend,
    zrecv,
    zedge,
    saved,
    raw,
    red_x,
    red_y,
    red_z,
    load_sem,
    store_sem,
    send_sem,
    recv_sem,
    red_send,
    red_recv,
):
    nx, ny, nz = sizes
    gx, gy, gz = lax.axis_index("gx"), lax.axis_index("gy"), lax.axis_index("gz")

    def device(dx, dy, dz):
        return {
            "gx": lax.rem(gx + (dx + nx), nx) if dx else gx,
            "gy": lax.rem(gy + (dy + ny), ny) if dy else gy,
            "gz": lax.rem(gz + (dz + nz), nz) if dz else gz,
        }

    loads = [
        pltpu.make_async_copy(design_hbm, design, load_sem.at[4]),
        pltpu.make_async_copy(labels_hbm, labels, load_sem.at[5]),
    ]
    slabs = {}
    for x in (0, 3, 1, 2):
        slabs[x] = pltpu.make_async_copy(pop_hbm.at[:, x], pop.at[x], load_sem.at[x])
    for copy in loads:
        copy.start()
    for x in (0, 3, 1, 2):
        slabs[x].start()

    barrier = pltpu.get_barrier_semaphore()
    partners = [n for n in NEIGHBOURS if sum(map(abs, n)) == 2]
    partners += [(k, 0, 0) for k in range(1, nx)]
    partners += [(0, k, 0) for k in range(1, ny)]
    partners += [(0, 0, k) for k in range(1, nz)]
    for partner in partners:
        pl.semaphore_signal(barrier, inc=1, device_id=device(*partner), device_id_type=MESH)

    lane = lax.broadcasted_iota(jnp.int32, (8, NZ), 1)
    first, last = lane == 0, lane == NZ - 1

    def exchange(turn):
        pad, zs, zr, ze = pads.at[turn], zsend.at[turn], zrecv.at[turn], zedge.at[turn]
        copies = {}
        for number, (dx, dy, dz) in enumerate(NEIGHBOURS):
            if dz == 0:
                if dx > 0:
                    xs, xd, group = 4, 0, slice(0, 5)
                elif dx < 0:
                    xs, xd, group = 1, 5, slice(8, 13)
                else:
                    xs, xd, group = slice(1, 5), slice(1, 5), slice(4, 9) if dy > 0 else slice(12, 17)
                if dy > 0:
                    ys, yd = slice(23, 24), slice(7, 8)
                elif dy < 0:
                    ys, yd = slice(8, 9), slice(24, 25)
                else:
                    ys, yd = slice(8, 24), slice(8, 24)
                if dx and dy:
                    group = SLOT[VELOCITY.index((dx, dy, dz))]
                src, dst = pad.at[xs, group, ys], pad.at[xd, group, yd]
            else:
                s = 0 if dz > 0 else 1
                if dx:
                    src, dst = zs.at[s], ze.at[s, 0 if dx > 0 else 1]
                elif dy > 0:
                    src, dst = zs.at[s, 15:16], zr.at[s, 7:8]
                elif dy < 0:
                    src, dst = zs.at[s, 0:1], zr.at[s, 24:25]
                else:
                    src, dst = zs.at[s], zr.at[s, 8:24]
            copies[(dx, dy, dz)] = pltpu.make_async_remote_copy(
                src_ref=src,
                dst_ref=dst,
                send_sem=send_sem.at[turn, number],
                recv_sem=recv_sem.at[turn, number],
                device_id=device(dx, dy, dz),
                device_id_type=MESH,
            )
        return copies

    exchanges = [exchange(turn) for turn in range(ROUNDS)]

    def send_x(turn):
        for (dx, dy, dz), copy in exchanges[turn].items():
            if dx and not dz:
                copy.start()

    def send_rest(turn):
        for (dx, dy, dz), copy in exchanges[turn].items():
            if not (dx and not dz):
                copy.start()

    def receive(turn):
        pad, zr, ze = pads.at[turn], zrecv.at[turn], zedge.at[turn]
        for copy in exchanges[turn].values():
            copy.wait_recv()

        @pl.when(gx == 0)
        def _():
            pad[0, 0:5, 7:25, :] = jnp.zeros((5, 18, NZ), F32)
            ze[:, 0] = jnp.zeros((2, NY, NZ), F32)

        @pl.when(gx == nx - 1)
        def _():
            pad[5, 8:13, 7:25, :] = jnp.zeros((5, 18, NZ), F32)
            ze[:, 1] = jnp.zeros((2, NY, NZ), F32)

        @pl.when(gy == 0)
        def _():
            pad[:, 4:9, 7:8, :] = jnp.zeros((6, 5, 1, NZ), F32)
            zr[:, 7:8, :] = jnp.zeros((2, 1, NZ), F32)

        @pl.when(gy == ny - 1)
        def _():
            pad[:, 12:17, 24:25, :] = jnp.zeros((6, 5, 1, NZ), F32)
            pad[0, 0:1, 24:25, :] = jnp.zeros((1, 1, NZ), F32)
            zr[:, 24:25, :] = jnp.zeros((2, 1, NZ), F32)

        @pl.when(gz == 0)
        def _():
            zr[0, 7:25, :] = jnp.zeros((18, NZ), F32)
            ze[0] = jnp.zeros((2, NY, NZ), F32)

        @pl.when(gz == nz - 1)
        def _():
            zr[1, 7:25, :] = jnp.zeros((18, NZ), F32)
            ze[1] = jnp.zeros((2, NY, NZ), F32)

        place = lane % 8
        for s in range(2):
            for h in range(HALVES):
                rows = slice(8 * h, 8 * h + 8)
                own = slice(8 * h + ROW, 8 * h + ROW + 8)
                below = pltpu.roll(ze[s, 0, rows, :], NZ - 4, 1)
                above = pltpu.roll(ze[s, 1, rows, :], 4, 1)
                zr[s, own, :] = jnp.where(
                    place == 0, below, jnp.where(place == 5, above, zr[s, own, :])
                )

    def gather(turn, x, h):
        values = []
        for index in range(19):
            cx, cy, cz = VELOCITY[index]
            slot = SLOT[index]
            if index == 9 and x > 0:
                slot = TWIN
            start = ROW + 8 * h - cy
            value = pads[turn, x + 1 - cx, slot, start : start + 8, :]
            if cz:
                s = 0 if cz > 0 else 1
                k = (ZPLUS if cz > 0 else ZMINUS).index(index)
                column = 8 * k + 1 + x - cx
                halo = zrecv[turn, s, start : start + 8, :]
                shift = (-column) % NZ if cz > 0 else NZ - 1 - column
                halo = pltpu.roll(halo, shift, 1) if shift else halo
                value = jnp.where(first if cz > 0 else last, halo, value)
            values.append(value)
        return values

    def scatter(turn, x, h, values, packed):
        rows = slice(ROW + 8 * h, ROW + 8 * h + 8)
        for index in range(19):
            cz = VELOCITY[index][2]
            value = values[index]
            if cz:
                s = 0 if cz > 0 else 1
                k = (ZPLUS if cz > 0 else ZMINUS).index(index)
                column = 8 * k + 1 + x
                shift = (column + 1) % NZ if cz > 0 else column
                packed[s][h] = jnp.where(lane == column, pltpu.roll(value, shift, 1), packed[s][h])
                value = pltpu.roll(value, 1 if cz > 0 else NZ - 1, 1)
            pads[turn, x + 1, SLOT[index], rows, :] = value
            if index == 9:
                pads[turn, x + 1, TWIN, rows, :] = value

    def stage(turn, block):
        zero = jnp.zeros((8, NZ), F32)
        packed = [[zero] * HALVES, [zero] * HALVES]
        for x in (0, 3):
            for h in range(HALVES):
                scatter(turn, x, h, block(x, h), packed)
        if turn == 0:
            pl.semaphore_wait(barrier, len(partners))
        send_x(turn)
        for x in (1, 2):
            for h in range(HALVES):
                scatter(turn, x, h, block(x, h), packed)
        for s in range(2):
            for h in range(HALVES):
                zsend[turn, s, 8 * h : 8 * h + 8, :] = packed[s][h]
        send_rest(turn)

    def moments(f):
        sums = {i: f[i] + f[i + 1] for i in PAIRS}
        diff = {i: f[i] - f[i + 1] for i in PAIRS}
        density = f[0] + (
            ((sums[1] + sums[3]) + (sums[5] + sums[7]))
            + ((sums[9] + sums[11]) + (sums[13] + (sums[15] + sums[17])))
        )
        jx = diff[1] + ((diff[7] + diff[9]) + (diff[11] + diff[13]))
        jy = diff[3] + ((diff[7] - diff[9]) + (diff[15] + diff[17]))
        jz = diff[5] + ((diff[11] - diff[13]) + (diff[15] - diff[17]))
        return density, jx, jy, jz

    def along(index, v):
        total = None
        for axis in range(3):
            c = VELOCITY[index][axis]
            if c:
                if total is None:
                    total = v[axis]
                else:
                    total = total + v[axis] if c > 0 else total - v[axis]
        return total

    def collide(which, f, x, h):
        rows = slice(8 * h, 8 * h + 8)
        mark = labels[x, rows, :]
        fluid, solid, inlet, outlet = mark == 1, mark == 2, mark == 3, mark == 4
        damping = 1.0 / (1.0 + design[x, rows, :])
        density, jx, jy, jz = moments(f)
        inverse = 1.0 / jnp.where(solid, 1.0, density)
        factor = inverse * jnp.where(fluid, damping, jnp.where(outlet, 1.0, 0.0))
        ux, uy, uz = jx * factor, jy * factor, jnp.where(inlet, INFLOW, jz * factor)
        saved[which, 0, x, rows, :] = ux
        saved[which, 1, x, rows, :] = uy
        saved[which, 2, x, rows, :] = uz
        saved[which, 3, x, rows, :] = jnp.where(
            fluid, RELAX * damping, jnp.where(outlet, inverse, 0.0)
        )
        saved[which, 4, x, rows, :] = jnp.where(fluid, -RELAX * damping * density, 0.0)
        weight = jnp.where(fluid, RELAX * density, 1.0)
        keep = jnp.where(fluid, 1.0 - RELAX, 0.0)
        rest = 1.0 - 1.5 * (ux * ux + uy * uy + uz * uz)
        wide, thin = weight * (1.0 / 18.0), weight * (1.0 / 36.0)
        post = [None] * 19
        post[0] = jnp.where(solid, f[0], keep * f[0] + (weight * (1.0 / 3.0)) * rest)
        for i in PAIRS:
            w = wide if i < 7 else thin
            cu = along(i, (ux, uy, uz))
            even = w * (rest + 4.5 * (cu * cu))
            odd = w * (3.0 * cu)
            post[i] = jnp.where(solid, f[i + 1], keep * f[i] + (even + odd))
            post[i + 1] = jnp.where(solid, f[i], keep * f[i + 1] + (even - odd))
        return post

    def transpose(which, g, x, h):
        rows = slice(8 * h, 8 * h + 8)
        mark = labels[x, rows, :]
        fluid, solid = mark == 1, mark == 2
        u = [saved[which, a, x, rows, :] for a in range(3)]
        gain, slope = saved[which, 3, x, rows, :], saved[which, 4, x, rows, :]
        ux, uy, uz = u
        s = {i: g[i] + g[i + 1] for i in PAIRS}
        d = {i: g[i] - g[i + 1] for i in PAIRS}
        wide, thin = 1.0 / 18.0, 1.0 / 36.0
        sxy, sxz, syz = s[7] + s[9], s[11] + s[13], s[15] + s[17]
        m0 = (
            (1.0 / 3.0) * g[0]
            + wide * (s[1] + s[3] + s[5])
            + thin * (sxy + sxz + syz)
        )
        m1x = wide * d[1] + thin * ((d[7] + d[9]) + (d[11] + d[13]))
        m1y = wide * d[3] + thin * ((d[7] - d[9]) + (d[15] + d[17]))
        m1z = wide * d[5] + thin * ((d[11] - d[13]) + (d[15] - d[17]))
        mxx = wide * s[1] + thin * (sxy + sxz)
        myy = wide * s[3] + thin * (sxy + syz)
        mzz = wide * s[5] + thin * (sxz + syz)
        mxy = thin * (s[7] - s[9])
        mxz = thin * (s[11] - s[13])
        myz = thin * (s[15] - s[17])
        hx = mxx * ux + mxy * uy + mxz * uz
        hy = mxy * ux + myy * uy + myz * uz
        hz = mxz * ux + myz * uy + mzz * uz
        quad = ux * hx + uy * hy + uz * hz
        square = ux * ux + uy * uy + uz * uz
        bx = 3.0 * (m1x - ux * m0) + 9.0 * hx
        by = 3.0 * (m1y - uy * m0) + 9.0 * hy
        bz = 3.0 * (m1z - uz * m0) + 9.0 * hz
        bu = bx * ux + by * uy + bz * uz
        base = jnp.where(
            fluid, RELAX * (m0 + 1.5 * square * m0 - 4.5 * quad), -(bu * gain)
        )
        e = (bx * gain, by * gain, bz * gain)
        keep = jnp.where(fluid, 1.0 - RELAX, 0.0)
        back = [None] * 19
        back[0] = jnp.where(solid, g[0], keep * g[0] + base)
        for i in PAIRS:
            ce = along(i, e)
            back[i] = jnp.where(solid, g[i + 1], keep * g[i] + (base + ce))
            back[i + 1] = jnp.where(solid, g[i], keep * g[i + 1] + (base - ce))
        return back, slope * bu

    def reverse(values):
        return [values[OPPOSITE[i]] for i in range(19)]

    for copy in loads:
        copy.wait()
    waited = set()

    def block_one(x, h):
        if x not in waited:
            slabs[x].wait()
            waited.add(x)
        f = [pop[x, i, 8 * h : 8 * h + 8, :] for i in range(19)]
        return collide(0, f, x, h)

    stage(0, block_one)

    receive(0)
    stage(1, lambda x, h: collide(1, gather(0, x, h), x, h))

    receive(1)
    lost = []

    def block_final(x, h):
        rows = slice(8 * h, 8 * h + 8)
        solidity = design[x, rows, :]
        fluid = labels[x, rows, :] == 1
        density, jx, jy, jz = moments(gather(1, x, h))
        inverse = jnp.where(fluid, 1.0 / jnp.where(fluid, density, 1.0), 0.0)
        v = (jx * inverse, jy * inverse, jz * inverse)
        square = v[0] * v[0] + v[1] * v[1] + v[2] * v[2]
        direct = 10.0 * density * square
        raw[x, rows, :] = direct
        lost.append(solidity * direct)
        base = -10.0 * solidity * square
        twice = 20.0 * solidity
        e = (twice * v[0], twice * v[1], twice * v[2])
        g = [base] * 19
        for i in PAIRS:
            ce = along(i, e)
            g[i], g[i + 1] = base + ce, base - ce
        return reverse(g)

    stage(2, block_final)

    receive(2)

    def block_two(x, h):
        rows = slice(8 * h, 8 * h + 8)
        back, sens = transpose(1, reverse(gather(2, x, h)), x, h)
        raw[x, rows, :] = raw[x, rows, :] + sens
        return reverse(back)

    stage(3, block_two)

    receive(3)
    sizes_of = jnp.zeros((8, NZ), F32)
    stores = []
    for x in range(NX):
        for h in range(HALVES):
            rows = slice(8 * h, 8 * h + 8)
            back, sens = transpose(0, reverse(gather(3, x, h)), x, h)
            total = raw[x, rows, :] + sens
            raw[x, rows, :] = total
            sizes_of = sizes_of + jnp.abs(total)
            for i in range(19):
                adj[x, i, rows, :] = back[i]
        stores.append(pltpu.make_async_copy(adj.at[x], adj_hbm.at[:, x], store_sem.at[x]))
        stores[-1].start()

    lost_of = lost[0]
    for term in lost[1:]:
        lost_of = lost_of + term
    row = lax.broadcasted_iota(jnp.int32, (8, NZ), 0)
    mine = jnp.where(
        row == 0,
        jnp.sum(lost_of, axis=0, keepdims=True),
        jnp.where(row == 1, jnp.sum(sizes_of, axis=0, keepdims=True), 0.0),
    )

    number = 0
    sent = []
    for buffer, me, count, step in (
        (red_z, gz, nz, (0, 0, 1)),
        (red_y, gy, ny, (0, 1, 0)),
        (red_x, gx, nx, (1, 0, 0)),
    ):
        buffer[me] = mine
        copies = []
        for k in range(1, count):
            copies.append(
                pltpu.make_async_remote_copy(
                    src_ref=buffer.at[me],
                    dst_ref=buffer.at[me],
                    send_sem=red_send.at[number],
                    recv_sem=red_recv.at[number],
                    device_id=device(*(k * c for c in step)),
                    device_id_type=MESH,
                )
            )
            number += 1
        for copy in copies:
            copy.start()
        for copy in copies:
            copy.wait_recv()
        sent += copies
        mine = buffer[0]
        for k in range(1, count):
            mine = mine + buffer[k]

    cells = NX * NY * NZ * nx * ny * nz
    loss = jnp.sum(jnp.where(row == 0, mine, 0.0))
    size = jnp.sum(jnp.where(row == 1, mine, 0.0))
    obj_ref[0] = 20.0 * loss / cells
    scale = size / cells + 1e-06
    inverse = 1.0 / jnp.full((8, NZ), scale, F32)
    for x in range(NX):
        for h in range(HALVES):
            rows = slice(8 * h, 8 * h + 8)
            sens_ref[x, rows, :] = raw[x, rows, :] * inverse

    for copy in stores:
        copy.wait()
    for copies in exchanges:
        for copy in copies.values():
            copy.wait_send()
    for copy in sent:
        copy.wait_send()


def solution(mesh):
    nx, ny, nz = (mesh.shape[a] for a in ("gx", "gy", "gz"))
    partners = nx + ny + nz - 3

    def body(populations, design, labels):
        cells = (NX, NY, NZ)
        adjoint, sensitivity, objective = pl.pallas_call(
            lambda *refs: kernel((nx, ny, nz), *refs),
            out_shape=(
                jax.ShapeDtypeStruct((19,) + cells, F32),
                jax.ShapeDtypeStruct(cells, F32),
                jax.ShapeDtypeStruct((1,), F32),
            ),
            in_specs=[pl.BlockSpec(memory_space=pl.ANY)] * 3,
            out_specs=(
                pl.BlockSpec(memory_space=pl.ANY),
                pl.BlockSpec(memory_space=pltpu.VMEM),
                pl.BlockSpec(memory_space=pltpu.SMEM),
            ),
            scratch_shapes=[
                pltpu.VMEM((NX, 19, NY, NZ), F32),
                pltpu.VMEM(cells, F32),
                pltpu.VMEM(cells, jnp.int32),
                pltpu.VMEM((NX, 19, NY, NZ), F32),
                pltpu.VMEM((ROUNDS, NX + 2, 20, NY + 16, NZ), F32),
                pltpu.VMEM((ROUNDS, 2, NY, NZ), F32),
                pltpu.VMEM((ROUNDS, 2, NY + 16, NZ), F32),
                pltpu.VMEM((ROUNDS, 2, 2, NY, NZ), F32),
                pltpu.VMEM((2, 5) + cells, F32),
                pltpu.VMEM(cells, F32),
                pltpu.VMEM((nx, 8, NZ), F32),
                pltpu.VMEM((ny, 8, NZ), F32),
                pltpu.VMEM((nz, 8, NZ), F32),
                pltpu.SemaphoreType.DMA((6,)),
                pltpu.SemaphoreType.DMA((NX,)),
                pltpu.SemaphoreType.DMA((ROUNDS, 18)),
                pltpu.SemaphoreType.DMA((ROUNDS, 18)),
                pltpu.SemaphoreType.DMA((partners,)),
                pltpu.SemaphoreType.DMA((partners,)),
            ],
            compiler_params=pltpu.CompilerParams(
                collective_id=0, has_side_effects=True, vmem_limit_bytes=40 * 1024 * 1024
            ),
            cost_estimate=pl.CostEstimate(
                flops=10_000_000, bytes_accessed=1_500_000, transcendentals=0
            ),
        )(populations, design, labels)
        return adjoint, sensitivity, objective.reshape(())

    in_specs = (P(None, "gx", "gy", "gz"), P("gx", "gy", "gz"), P("gx", "gy", "gz"))
    out_specs = (P(None, "gx", "gy", "gz"), P("gx", "gy", "gz"), P())
    return jax.shard_map(body, mesh=mesh, in_specs=in_specs, out_specs=out_specs, check_vma=False)
```

time: 299 us -> 48.1 us (0.16)
  blocking collectives: 80.5 us -> 0 us
  starting transfers between devices: 74 us -> 0 us
  other arithmetic: 67.4 us -> 0 us
  Pallas kernels: 0 us -> 41.4 us
  local copies, waits for them, and re-layouts: 43.4 us -> 4.03 us
  waiting for transfers between devices: 25.9 us -> 0 us
  between operations: 5.88 us -> 2.39 us
    psum x1 -> x0, blocking collectives: 80.5 us -> none  [body(): totals = lax.psum((local_total, jnp.sum(jnp.abs(raw))), ('gx', 'gy', 'gz'))]
    ppermute x24 -> x0, starting transfers between devices: 74 us -> none  [the longest x12 56 us: padded_2(): lax.ppermute(tail, axis, [(i, (i + 1) % count) for i in range(ends)])]
    unnamed x106 -> x0, other arithmetic: 46.5 us -> none
    pallas_call x0 -> x1, Pallas kernels: none -> 41.4 us  [body(): pl.pallas_call(lambda *refs: kernel((nx, ny, nz), *refs), out_shape=(jax....]
    ppermute x24 -> x0, waiting for transfers between devices: 25.9 us -> none  [the longest x12 21.2 us: padded_2(): lax.ppermute(head, axis, [((i + 1) % count, i) for i in range(ends)])]
    slice x16 -> x0, local copies, waits for them, and re-layouts: 20.1 us -> none  [the longest x10 11.6 us: padded_2(): lax.slice_in_dim(cells, cells.shape[dim] - width, cells.shape[dim], axis=...]
    ppermute x8 -> x0, local copies, waits for them, and re-layouts: 14.9 us -> none  [the longest x4 8.03 us: padded_2(): lax.ppermute(tail, axis, [(i, (i + 1) % count) for i in range(ends)])]
    select_n x6 -> x0, other arithmetic: 5.56 us -> none  [the longest x2 2.62 us: collide(): result = jnp.where(marks == 2, bounce, result)]
  transfers between devices with their start and end apart: 24 -> 0, of which waited for: 11 -> 0; matrix products, arithmetic and copies ran while one was open for 7% -> 0% of each run, Pallas kernels for 0% -> 0%
where the time goes in v1:
time: 48.1 us; the launch traced here: 47.8 us
  Pallas kernels  41.4 us (86%)
  local copies, waits for them, and re-layouts  4.03 us (8%)
  between operations  2.39 us (5%)
    pallas_call x1, Pallas kernels, body(): pl.pallas_call(lambda *refs: kernel((nx, ny, nz), *refs), out_shape=(jax....  41.4 us
    unnamed x8, local copies, waits for them, and re-layouts  4.03 us

profile of v1, /device:TPU:1, one launch (start us, length us, event | category | flops | bytes accessed | tf_op | source)
XLA Modules:
  0.0 47.8 jit_solution(6167517331224202866)
XLA Ops:
  0.6 0.0 copy-start
  0.6 1.1 %copy-done = f32[19,4,16,128]{3,2,1,0:T(8,128)S(1)} copy-done((f32[19,4,16,128]{3,2,1,0:T(8,128)S(1)}, f32[19,4,16,128]{3,2,1,0:T(8,128)}, u32[]{:S(2)}) %copy-start) | copy-done | bytes 622616
  1.7 0.0 copy-start.1
  1.7 0.8 %copy-done.1 = f32[4,16,128]{2,1,0:T(8,128)S(1)} copy-done((f32[4,16,128]{2,1,0:T(8,128)S(1)}, f32[4,16,128]{2,1,0:T(8,128)}, u32[]{:S(2)}) %copy-start.1) | copy-done | bytes 32792
  2.5 0.0 copy-start.2
  2.5 0.8 %copy-done.2 = s32[4,16,128]{2,1,0:T(8,128)S(1)} copy-done((s32[4,16,128]{2,1,0:T(8,128)S(1)}, s32[4,16,128]{2,1,0:T(8,128)}, u32[]{:S(2)}) %copy-start.2) | copy-done | bytes 32792
  3.2 41.4 %shard_map.58 = (f32[19,4,16,128]{3,2,1,0:T(8,128)S(1)}, f32[4,16,128]{2,1,0:T(8,128)S(1)}, f32[1]{0:T(128)}) custom-call(f32[19,4,16,128]{3,2,1,0:T(8,128)S(1)} %copy-done, f32[4,16,128]{2,1,0:T(8,128)S(1)} %copy-done.1, s32[4,16,128]{2,1,0:T(8,128)S(1)} %copy-done.2), custom_call_target="tpu_custom_call" | custom-call | flops 10000000 | bytes 1500000 | tf_op jit(solution)/shard_map/pallas_call | solution.py:507
  44.7 0.8 %copy.9 = f32[19,4,16,128]{3,2,1,0:T(8,128)} copy(f32[19,4,16,128]{3,2,1,0:T(8,128)S(1)} %get-tuple-element.12) | data formatting | bytes 1245184
  45.5 0.6 %copy.10 = f32[4,16,128]{2,1,0:T(8,128)} copy(f32[4,16,128]{2,1,0:T(8,128)S(1)} %get-tuple-element.13) | data formatting | bytes 65536
Async XLA Ops:
  0.6 1.1 %copy-start = (f32[19,4,16,128]{3,2,1,0:T(8,128)S(1)}, f32[19,4,16,128]{3,2,1,0:T(8,128)}, u32[]{:S(2)}) copy-start(f32[19,4,16,128]{3,2,1,0:T(8,128)} %refs_0_.1) | copy-start | bytes 1867780
  1.7 0.8 %copy-start.1 = (f32[4,16,128]{2,1,0:T(8,128)S(1)}, f32[4,16,128]{2,1,0:T(8,128)}, u32[]{:S(2)}) copy-start(f32[4,16,128]{2,1,0:T(8,128)} %refs_1_.1) | copy-start | bytes 98308
  2.5 0.8 %copy-start.2 = (s32[4,16,128]{2,1,0:T(8,128)S(1)}, s32[4,16,128]{2,1,0:T(8,128)}, u32[]{:S(2)}) copy-start(s32[4,16,128]{2,1,0:T(8,128)} %refs_2_.1) | copy-start | bytes 98308

commit v2 on v1

--- a/solution.py
+++ b/solution.py
@@ -43,6 +43,7 @@
 NX, NY, NZ = 4, 16, 128
 HALVES = NY // 8
 ROUNDS = 4
+PIECES = 4
 
 
 def neighbours():
@@ -61,8 +62,8 @@
     design_hbm,
     labels_hbm,
     adj_hbm,
-    sens_ref,
-    obj_ref,
+    raw_hbm,
+    sums_ref,
     pop,
     design,
     labels,
@@ -73,9 +74,8 @@
     zedge,
     saved,
     raw,
-    red_x,
+    red_p,
     red_y,
-    red_z,
     load_sem,
     store_sem,
     send_sem,
@@ -92,6 +92,20 @@
             "gy": lax.rem(gy + (dy + ny), ny) if dy else gy,
             "gz": lax.rem(gz + (dz + nz), nz) if dz else gz,
         }
+
+    inside = {
+        "gx": (gx > 0, gx < nx - 1),
+        "gy": (gy > 0, gy < ny - 1),
+        "gz": (gz > 0, gz < nz - 1),
+    }
+
+    def exists(dx, dy, dz):
+        found = None
+        for axis, d in (("gx", dx), ("gy", dy), ("gz", dz)):
+            if d:
+                here = inside[axis][1 if d > 0 else 0]
+                found = here if found is None else found & here
+        return found
 
     loads = [
         pltpu.make_async_copy(design_hbm, design, load_sem.at[4]),
@@ -105,11 +119,41 @@
     for x in (0, 3, 1, 2):
         slabs[x].start()
 
+    @pl.when(gx == 0)
+    def _():
+        pads[:, 0, 0:5, 7:25, :] = jnp.zeros((ROUNDS, 5, 18, NZ), F32)
+        zedge[:, :, 0] = jnp.zeros((ROUNDS, 2, NY, NZ), F32)
+
+    @pl.when(gx == nx - 1)
+    def _():
+        pads[:, 5, 8:13, 7:25, :] = jnp.zeros((ROUNDS, 5, 18, NZ), F32)
+        zedge[:, :, 1] = jnp.zeros((ROUNDS, 2, NY, NZ), F32)
+
+    @pl.when(gy == 0)
+    def _():
+        pads[:, :, 4:9, 7:8, :] = jnp.zeros((ROUNDS, NX + 2, 5, 1, NZ), F32)
+        zrecv[:, :, 7:8, :] = jnp.zeros((ROUNDS, 2, 1, NZ), F32)
+
+    @pl.when(gy == ny - 1)
+    def _():
+        pads[:, :, 12:17, 24:25, :] = jnp.zeros((ROUNDS, NX + 2, 5, 1, NZ), F32)
+        pads[:, 0, 0:1, 24:25, :] = jnp.zeros((ROUNDS, 1, 1, NZ), F32)
+        zrecv[:, :, 24:25, :] = jnp.zeros((ROUNDS, 2, 1, NZ), F32)
+
+    @pl.when(gz == 0)
+    def _():
+        zrecv[:, 0, 7:25, :] = jnp.zeros((ROUNDS, 18, NZ), F32)
+        zedge[:, 0] = jnp.zeros((ROUNDS, 2, NY, NZ), F32)
+
+    @pl.when(gz == nz - 1)
+    def _():
+        zrecv[:, 1, 7:25, :] = jnp.zeros((ROUNDS, 18, NZ), F32)
+        zedge[:, 1] = jnp.zeros((ROUNDS, 2, NY, NZ), F32)
+
     barrier = pltpu.get_barrier_semaphore()
-    partners = [n for n in NEIGHBOURS if sum(map(abs, n)) == 2]
-    partners += [(k, 0, 0) for k in range(1, nx)]
-    partners += [(0, k, 0) for k in range(1, ny)]
-    partners += [(0, 0, k) for k in range(1, nz)]
+    plane = [(a, 0, b) for a in range(nx) for b in range(nz) if a or b]
+    column = [(0, k, 0) for k in range(1, ny)]
+    partners = [n for n in NEIGHBOURS if n[1] and (n[0] or n[2])] + plane + column
     for partner in partners:
         pl.semaphore_signal(barrier, inc=1, device_id=device(*partner), device_id_type=MESH)
 
@@ -161,48 +205,17 @@
     def send_x(turn):
         for (dx, dy, dz), copy in exchanges[turn].items():
             if dx and not dz:
-                copy.start()
+                pl.when(exists(dx, dy, dz))(copy.start)
 
     def send_rest(turn):
-        for (dx, dy, dz), copy in exchanges[turn].items():
-            if not (dx and not dz):
-                copy.start()
+        rest = [item for item in exchanges[turn].items() if item[0][2] or not item[0][0]]
+        for (dx, dy, dz), copy in sorted(rest, key=lambda item: not item[0][1]):
+            pl.when(exists(dx, dy, dz))(copy.start)
 
     def receive(turn):
         pad, zr, ze = pads.at[turn], zrecv.at[turn], zedge.at[turn]
-        for copy in exchanges[turn].values():
-            copy.wait_recv()
-
-        @pl.when(gx == 0)
-        def _():
-            pad[0, 0:5, 7:25, :] = jnp.zeros((5, 18, NZ), F32)
-            ze[:, 0] = jnp.zeros((2, NY, NZ), F32)
-
-        @pl.when(gx == nx - 1)
-        def _():
-            pad[5, 8:13, 7:25, :] = jnp.zeros((5, 18, NZ), F32)
-            ze[:, 1] = jnp.zeros((2, NY, NZ), F32)
-
-        @pl.when(gy == 0)
-        def _():
-            pad[:, 4:9, 7:8, :] = jnp.zeros((6, 5, 1, NZ), F32)
-            zr[:, 7:8, :] = jnp.zeros((2, 1, NZ), F32)
-
-        @pl.when(gy == ny - 1)
-        def _():
-            pad[:, 12:17, 24:25, :] = jnp.zeros((6, 5, 1, NZ), F32)
-            pad[0, 0:1, 24:25, :] = jnp.zeros((1, 1, NZ), F32)
-            zr[:, 24:25, :] = jnp.zeros((2, 1, NZ), F32)
-
-        @pl.when(gz == 0)
-        def _():
-            zr[0, 7:25, :] = jnp.zeros((18, NZ), F32)
-            ze[0] = jnp.zeros((2, NY, NZ), F32)
-
-        @pl.when(gz == nz - 1)
-        def _():
-            zr[1, 7:25, :] = jnp.zeros((18, NZ), F32)
-            ze[1] = jnp.zeros((2, NY, NZ), F32)
+        for (dx, dy, dz), copy in exchanges[turn].items():
+            pl.when(exists(-dx, -dy, -dz))(copy.wait_recv)
 
         place = lane % 8
         for s in range(2):
@@ -425,18 +438,13 @@
 
     receive(3)
     sizes_of = jnp.zeros((8, NZ), F32)
-    stores = []
     for x in range(NX):
         for h in range(HALVES):
             rows = slice(8 * h, 8 * h + 8)
-            back, sens = transpose(0, reverse(gather(3, x, h)), x, h)
+            _, sens = transpose(0, reverse(gather(3, x, h)), x, h)
             total = raw[x, rows, :] + sens
             raw[x, rows, :] = total
             sizes_of = sizes_of + jnp.abs(total)
-            for i in range(19):
-                adj[x, i, rows, :] = back[i]
-        stores.append(pltpu.make_async_copy(adj.at[x], adj_hbm.at[:, x], store_sem.at[x]))
-        stores[-1].start()
 
     lost_of = lost[0]
     for term in lost[1:]:
@@ -448,73 +456,114 @@
         jnp.where(row == 1, jnp.sum(sizes_of, axis=0, keepdims=True), 0.0),
     )
 
-    number = 0
-    sent = []
-    for buffer, me, count, step in (
-        (red_z, gz, nz, (0, 0, 1)),
-        (red_y, gy, ny, (0, 1, 0)),
-        (red_x, gx, nx, (1, 0, 0)),
-    ):
+    def spread(buffer, me, steps, base):
         buffer[me] = mine
         copies = []
-        for k in range(1, count):
+        for number, step in enumerate(steps):
             copies.append(
                 pltpu.make_async_remote_copy(
                     src_ref=buffer.at[me],
                     dst_ref=buffer.at[me],
-                    send_sem=red_send.at[number],
-                    recv_sem=red_recv.at[number],
-                    device_id=device(*(k * c for c in step)),
+                    send_sem=red_send.at[base + number],
+                    recv_sem=red_recv.at[base + number],
+                    device_id=device(*step),
                     device_id_type=MESH,
                 )
             )
-            number += 1
         for copy in copies:
             copy.start()
+        return copies
+
+    def added(buffer, copies):
         for copy in copies:
             copy.wait_recv()
-        sent += copies
-        mine = buffer[0]
-        for k in range(1, count):
-            mine = mine + buffer[k]
+        terms = [buffer[k] for k in range(len(copies) + 1)]
+        while len(terms) > 1:
+            terms = [a + b for a, b in zip(terms[::2], terms[1::2])]
+        return terms[0]
+
+    sent = spread(red_p, gx * nz + gz, plane, 0)
+    stores = [pltpu.make_async_copy(raw, raw_hbm, store_sem.at[NX])]
+    stores[0].start()
+    for x in range(NX):
+        for h in range(HALVES):
+            rows = slice(8 * h, 8 * h + 8)
+            back, _ = transpose(0, reverse(gather(3, x, h)), x, h)
+            for i in range(19):
+                adj[x, i, rows, :] = back[i]
+        stores.append(pltpu.make_async_copy(adj.at[x], adj_hbm.at[:, x], store_sem.at[x]))
+        stores[-1].start()
+    for turn in range(ROUNDS):
+        for (dx, dy, dz), copy in exchanges[turn].items():
+            pl.when(exists(dx, dy, dz))(copy.wait_send)
+    mine = added(red_p, sent)
+    last_sent = spread(red_y, gy, column, len(plane))
+    mine = added(red_y, last_sent)
+    sent = sent + last_sent
 
     cells = NX * NY * NZ * nx * ny * nz
     loss = jnp.sum(jnp.where(row == 0, mine, 0.0))
     size = jnp.sum(jnp.where(row == 1, mine, 0.0))
-    obj_ref[0] = 20.0 * loss / cells
-    scale = size / cells + 1e-06
-    inverse = 1.0 / jnp.full((8, NZ), scale, F32)
+    sums_ref[0] = 20.0 * loss / cells
+    sums_ref[1] = size / cells + 1e-06
+
+    for copy in sent:
+        copy.wait_send()
+    for copy in stores:
+        copy.wait()
+
+
+def finish(sums_in, adj_in, raw_in, adj_out, sens_out, obj_out, raw, adj, sums, sem):
+    cuts = [19 * k // PIECES for k in range(PIECES + 1)]
+    loads = [
+        pltpu.make_async_copy(sums_in, sums, sem.at[2 * PIECES]),
+        pltpu.make_async_copy(raw_in, raw, sem.at[2 * PIECES + 1]),
+    ]
+    coming, going = [], []
+    for k in range(PIECES):
+        part = slice(cuts[k], cuts[k + 1])
+        coming.append(pltpu.make_async_copy(adj_in.at[part], adj.at[part], sem.at[k]))
+        going.append(
+            pltpu.make_async_copy(adj.at[part], adj_out.at[part], sem.at[PIECES + k])
+        )
+        coming[k].start()
+    for copy in loads:
+        copy.start()
+    for k in range(PIECES):
+        coming[k].wait()
+        going[k].start()
+    for copy in loads:
+        copy.wait()
+    obj_out[0] = sums[0]
+    inverse = 1.0 / jnp.full((8, NZ), sums[1], F32)
     for x in range(NX):
         for h in range(HALVES):
             rows = slice(8 * h, 8 * h + 8)
-            sens_ref[x, rows, :] = raw[x, rows, :] * inverse
-
-    for copy in stores:
-        copy.wait()
-    for copies in exchanges:
-        for copy in copies.values():
-            copy.wait_send()
-    for copy in sent:
-        copy.wait_send()
+            raw[x, rows, :] = raw[x, rows, :] * inverse
+    store = pltpu.make_async_copy(raw, sens_out, sem.at[2 * PIECES + 2])
+    store.start()
+    for k in range(PIECES):
+        going[k].wait()
+    store.wait()
 
 
 def solution(mesh):
     nx, ny, nz = (mesh.shape[a] for a in ("gx", "gy", "gz"))
-    partners = nx + ny + nz - 3
+    partners = nx * nz + ny - 2
 
     def body(populations, design, labels):
         cells = (NX, NY, NZ)
-        adjoint, sensitivity, objective = pl.pallas_call(
+        adjoint, raw, sums = pl.pallas_call(
             lambda *refs: kernel((nx, ny, nz), *refs),
             out_shape=(
                 jax.ShapeDtypeStruct((19,) + cells, F32),
                 jax.ShapeDtypeStruct(cells, F32),
-                jax.ShapeDtypeStruct((1,), F32),
+                jax.ShapeDtypeStruct((2,), F32),
             ),
-            in_specs=[pl.BlockSpec(memory_space=pl.ANY)] * 3,
+            in_specs=[pl.BlockSpec(memory_space=pltpu.HBM)] * 3,
             out_specs=(
-                pl.BlockSpec(memory_space=pl.ANY),
-                pl.BlockSpec(memory_space=pltpu.VMEM),
+                pl.BlockSpec(memory_space=pltpu.HBM),
+                pl.BlockSpec(memory_space=pltpu.HBM),
                 pl.BlockSpec(memory_space=pltpu.SMEM),
             ),
             scratch_shapes=[
@@ -528,23 +577,47 @@
                 pltpu.VMEM((ROUNDS, 2, 2, NY, NZ), F32),
                 pltpu.VMEM((2, 5) + cells, F32),
                 pltpu.VMEM(cells, F32),
-                pltpu.VMEM((nx, 8, NZ), F32),
+                pltpu.VMEM((nx * nz, 8, NZ), F32),
                 pltpu.VMEM((ny, 8, NZ), F32),
-                pltpu.VMEM((nz, 8, NZ), F32),
                 pltpu.SemaphoreType.DMA((6,)),
-                pltpu.SemaphoreType.DMA((NX,)),
+                pltpu.SemaphoreType.DMA((NX + 1,)),
                 pltpu.SemaphoreType.DMA((ROUNDS, 18)),
                 pltpu.SemaphoreType.DMA((ROUNDS, 18)),
                 pltpu.SemaphoreType.DMA((partners,)),
                 pltpu.SemaphoreType.DMA((partners,)),
             ],
             compiler_params=pltpu.CompilerParams(
-                collective_id=0, has_side_effects=True, vmem_limit_bytes=40 * 1024 * 1024
+                collective_id=0, has_side_effects=True, vmem_limit_bytes=60 * 1024 * 1024
             ),
             cost_estimate=pl.CostEstimate(
                 flops=10_000_000, bytes_accessed=1_500_000, transcendentals=0
             ),
         )(populations, design, labels)
+        adjoint, sensitivity, objective = pl.pallas_call(
+            finish,
+            out_shape=(
+                jax.ShapeDtypeStruct((19,) + cells, F32),
+                jax.ShapeDtypeStruct(cells, F32),
+                jax.ShapeDtypeStruct((1,), F32),
+            ),
+            in_specs=[
+                pl.BlockSpec(memory_space=pltpu.HBM),
+                pl.BlockSpec(memory_space=pltpu.HBM),
+                pl.BlockSpec(memory_space=pltpu.HBM),
+            ],
+            out_specs=(
+                pl.BlockSpec(memory_space=pltpu.HBM),
+                pl.BlockSpec(memory_space=pltpu.HBM),
+                pl.BlockSpec(memory_space=pltpu.SMEM),
+            ),
+            scratch_shapes=[
+                pltpu.VMEM(cells, F32),
+                pltpu.VMEM((19,) + cells, F32),
+                pltpu.SMEM((2,), F32),
+                pltpu.SemaphoreType.DMA((2 * PIECES + 3,)),
+            ],
+            compiler_params=pltpu.CompilerParams(vmem_limit_bytes=60 * 1024 * 1024),
+        )(sums, adjoint, raw)
         return adjoint, sensitivity, objective.reshape(())
 
     in_specs = (P(None, "gx", "gy", "gz"), P("gx", "gy", "gz"), P("gx", "gy", "gz"))

time: 48.1 us -> 42.5 us (0.88)
  local copies, waits for them, and re-layouts: 4.03 us -> 0 us
  between operations: 2.39 us -> 0.64 us
    unnamed x8 -> x0, local copies, waits for them, and re-layouts: 4.03 us -> none
    pallas_call x0 -> x1, Pallas kernels: none -> 2.42 us  [body(): pl.pallas_call(finish, out_shape=(jax.ShapeDtypeStruct((19,) + cells, F32...]
    pallas_call x1, Pallas kernels: 41.4 us -> 39.4 us  [body(): pl.pallas_call(lambda *refs: kernel((nx, ny, nz), *refs), out_shape=(jax....]
where the time goes in v2:
time: 42.5 us; the launch traced here: 42.4 us
  Pallas kernels  41.8 us (98%)
  between operations  0.64 us (2%)
    pallas_call x1, Pallas kernels, body(): pl.pallas_call(lambda *refs: kernel((nx, ny, nz), *refs), out_shape=(jax....  39.4 us
    pallas_call x1, Pallas kernels, body(): pl.pallas_call(finish, out_shape=(jax.ShapeDtypeStruct((19,) + cells, F32...  2.42 us

profile of v2, /device:TPU:1, one launch (start us, length us, event | category | flops | bytes accessed | tf_op | source)
XLA Modules:
  0.0 42.4 jit_solution(7346316353035346599)
XLA Ops:
  0.6 39.4 %shard_map.58 = (f32[19,4,16,128]{3,2,1,0:T(8,128)}, f32[4,16,128]{2,1,0:T(8,128)}, f32[2]{0:T(128)}) custom-call(f32[19,4,16,128]{3,2,1,0:T(8,128)} %refs_0_.1, f32[4,16,128]{2,1,0:T(8,128)} %refs_1_.1, s32[4,16,128]{2,1,0:T(8,128)} %refs_2_.1), custom_call_target="tpu_custom_call" | custom-call | flops 10000000 | bytes 1500000 | tf_op jit(solution)/shard_map/pallas_call | solution.py:556
  40.0 2.4 %shard_map.59 = (f32[19,4,16,128]{3,2,1,0:T(8,128)}, f32[4,16,128]{2,1,0:T(8,128)}, f32[1]{0:T(128)}) custom-call(f32[2]{0:T(128)} %get-tuple-element.9.sums_in, f32[19,4,16,128]{3,2,1,0:T(8,128)} %get-tuple-element.10.adj_in, f32[4,16,128]{2,1,0:T(8,128)} %get-tuple-element.11.raw_in), custom_call_target="tpu_custom_call" | custom-call | tf_op jit(solution)/shard_map/pallas_call | solution.py:596

commit v3 on v2

--- a/solution.py
+++ b/solution.py
@@ -158,7 +158,6 @@
         pl.semaphore_signal(barrier, inc=1, device_id=device(*partner), device_id_type=MESH)
 
     lane = lax.broadcasted_iota(jnp.int32, (8, NZ), 1)
-    first, last = lane == 0, lane == NZ - 1
 
     def exchange(turn):
         pad, zs, zr, ze = pads.at[turn], zsend.at[turn], zrecv.at[turn], zedge.at[turn]
@@ -213,20 +212,12 @@
             pl.when(exists(dx, dy, dz))(copy.start)
 
     def receive(turn):
-        pad, zr, ze = pads.at[turn], zrecv.at[turn], zedge.at[turn]
         for (dx, dy, dz), copy in exchanges[turn].items():
             pl.when(exists(-dx, -dy, -dz))(copy.wait_recv)
 
-        place = lane % 8
-        for s in range(2):
-            for h in range(HALVES):
-                rows = slice(8 * h, 8 * h + 8)
-                own = slice(8 * h + ROW, 8 * h + ROW + 8)
-                below = pltpu.roll(ze[s, 0, rows, :], NZ - 4, 1)
-                above = pltpu.roll(ze[s, 1, rows, :], 4, 1)
-                zr[s, own, :] = jnp.where(
-                    place == 0, below, jnp.where(place == 5, above, zr[s, own, :])
-                )
+    def column_of(index, x):
+        names = ZPLUS if VELOCITY[index][2] > 0 else ZMINUS
+        return 8 * names.index(index) + 1 + x
 
     def gather(turn, x, h):
         values = []
@@ -239,12 +230,13 @@
             value = pads[turn, x + 1 - cx, slot, start : start + 8, :]
             if cz:
                 s = 0 if cz > 0 else 1
-                k = (ZPLUS if cz > 0 else ZMINUS).index(index)
-                column = 8 * k + 1 + x - cx
-                halo = zrecv[turn, s, start : start + 8, :]
-                shift = (-column) % NZ if cz > 0 else NZ - 1 - column
-                halo = pltpu.roll(halo, shift, 1) if shift else halo
-                value = jnp.where(first if cz > 0 else last, halo, value)
+                column = column_of(index, (x - cx) % NX)
+                if 0 <= x - cx < NX:
+                    halo = zrecv[turn, s, start : start + 8, :]
+                else:
+                    halo = zedge[turn, s, 0 if cx > 0 else 1, 8 * h : 8 * h + 8, :]
+                value = jnp.where(lane == column, halo, value)
+                value = pltpu.roll(value, NZ - column if cz > 0 else NZ - 1 - column, 1)
             values.append(value)
         return values
 
@@ -255,11 +247,9 @@
             value = values[index]
             if cz:
                 s = 0 if cz > 0 else 1
-                k = (ZPLUS if cz > 0 else ZMINUS).index(index)
-                column = 8 * k + 1 + x
-                shift = (column + 1) % NZ if cz > 0 else column
-                packed[s][h] = jnp.where(lane == column, pltpu.roll(value, shift, 1), packed[s][h])
-                value = pltpu.roll(value, 1 if cz > 0 else NZ - 1, 1)
+                column = column_of(index, x)
+                value = pltpu.roll(value, column + 1 if cz > 0 else column, 1)
+                packed[s][h] = jnp.where(lane == column, value, packed[s][h])
             pads[turn, x + 1, SLOT[index], rows, :] = value
             if index == 9:
                 pads[turn, x + 1, TWIN, rows, :] = value

time: 42.5 us -> 42.1 us (level)
  Pallas kernels: 41.8 us -> 41.3 us
    pallas_call x1, Pallas kernels: 39.4 us -> 38.9 us  [body(): pl.pallas_call(lambda *refs: kernel((nx, ny, nz), *refs), out_shape=(jax....]
where the time goes in v3:
time: 42.1 us; the launch traced here: 42 us
  Pallas kernels  41.3 us (98%)
  between operations  0.64 us (2%)
    pallas_call x1, Pallas kernels, body(): pl.pallas_call(lambda *refs: kernel((nx, ny, nz), *refs), out_shape=(jax....  38.9 us
    pallas_call x1, Pallas kernels, body(): pl.pallas_call(finish, out_shape=(jax.ShapeDtypeStruct((19,) + cells, F32...  2.42 us

profile of v3, /device:TPU:1, one launch (start us, length us, event | category | flops | bytes accessed | tf_op | source)
XLA Modules:
  0.0 42.0 jit_solution(17515964310457682145)
XLA Ops:
  0.6 38.9 %shard_map.58 = (f32[19,4,16,128]{3,2,1,0:T(8,128)}, f32[4,16,128]{2,1,0:T(8,128)}, f32[2]{0:T(128)}) custom-call(f32[19,4,16,128]{3,2,1,0:T(8,128)} %refs_0_.1, f32[4,16,128]{2,1,0:T(8,128)} %refs_1_.1, s32[4,16,128]{2,1,0:T(8,128)} %refs_2_.1), custom_call_target="tpu_custom_call" | custom-call | flops 10000000 | bytes 1500000 | tf_op jit(solution)/shard_map/pallas_call | solution.py:546
  39.5 2.4 %shard_map.59 = (f32[19,4,16,128]{3,2,1,0:T(8,128)}, f32[4,16,128]{2,1,0:T(8,128)}, f32[1]{0:T(128)}) custom-call(f32[2]{0:T(128)} %get-tuple-element.9.sums_in, f32[19,4,16,128]{3,2,1,0:T(8,128)} %get-tuple-element.10.adj_in, f32[4,16,128]{2,1,0:T(8,128)} %get-tuple-element.11.raw_in), custom_call_target="tpu_custom_call" | custom-call | tf_op jit(solution)/shard_map/pallas_call | solution.py:586

commit v4 on v3

--- a/solution.py
+++ b/solution.py
@@ -37,7 +37,7 @@
 SLOT = {index: ORDER.index(index) for index in range(19)}
 TWIN = 16
 ZPLUS = [5, 11, 14, 15, 18]
-ZMINUS = [6, 12, 13, 16, 17]
+ZMINUS = [6, 13, 12, 17, 16]
 ROW = 8
 
 NX, NY, NZ = 4, 16, 128
@@ -74,12 +74,25 @@
     zedge,
     saved,
     raw,
+    part,
+    tile,
+    zpart,
+    from_x,
+    from_y,
+    from_xy,
+    from_plane,
+    from_z,
+    drag,
     red_p,
     red_y,
     load_sem,
     store_sem,
     send_sem,
     recv_sem,
+    part_send,
+    part_recv,
+    drag_send,
+    drag_recv,
     red_send,
     red_recv,
 ):
@@ -150,14 +163,38 @@
         zrecv[:, 1, 7:25, :] = jnp.zeros((ROUNDS, 18, NZ), F32)
         zedge[:, 1] = jnp.zeros((ROUNDS, 2, NY, NZ), F32)
 
+    from_y[...] = jnp.zeros(from_y.shape, F32)
+    from_xy[...] = jnp.zeros(from_xy.shape, F32)
+    from_plane[...] = jnp.zeros(from_plane.shape, F32)
+    from_z[...] = jnp.zeros(from_z.shape, F32)
+    drag[...] = jnp.zeros(drag.shape, F32)
+    zpart[7:8, :] = jnp.zeros((1, NZ), F32)
+    zpart[24:25, :] = jnp.zeros((1, NZ), F32)
+    pads[1, 1:5, 4:9, 7:8, :] = jnp.zeros((NX, 5, 1, NZ), F32)
+    pads[1, 1:5, 12:17, 24:25, :] = jnp.zeros((NX, 5, 1, NZ), F32)
+
+    @pl.when(gx == 0)
+    def _():
+        from_x[0] = jnp.zeros((4, 2, NY + 16, NZ), F32)
+
+    @pl.when(gx == nx - 1)
+    def _():
+        from_x[1] = jnp.zeros((4, 2, NY + 16, NZ), F32)
+
     barrier = pltpu.get_barrier_semaphore()
     plane = [(a, 0, b) for a in range(nx) for b in range(nz) if a or b]
-    column = [(0, k, 0) for k in range(1, ny)]
-    partners = [n for n in NEIGHBOURS if n[1] and (n[0] or n[2])] + plane + column
+    line = [(0, k, 0) for k in range(1, ny)]
+    corners = [(a, b, c) for a in (1, -1) for b in (1, -1) for c in (1, -1)]
+    partners = [n for n in NEIGHBOURS if n[1] and (n[0] or n[2])] + corners + plane + line
     for partner in partners:
         pl.semaphore_signal(barrier, inc=1, device_id=device(*partner), device_id_type=MESH)
 
     lane = lax.broadcasted_iota(jnp.int32, (8, NZ), 1)
+    half = lane // 2
+    place = half % 8
+    even = lane % 2 == 0
+    first, last = lane == 0, lane == NZ - 1
+    ends = first | last
 
     def exchange(turn):
         pad, zs, zr, ze = pads.at[turn], zsend.at[turn], zrecv.at[turn], zedge.at[turn]
@@ -199,7 +236,72 @@
             )
         return copies
 
-    exchanges = [exchange(turn) for turn in range(ROUNDS)]
+    exchanges = {turn: exchange(turn) for turn in (0, 3)}
+
+    def part_copies():
+        copies = {}
+
+        def copy(key, src, dst):
+            number = len(copies)
+            copies[key] = pltpu.make_async_remote_copy(
+                src_ref=src,
+                dst_ref=dst,
+                send_sem=part_send.at[number],
+                recv_sem=part_recv.at[number],
+                device_id=device(*key[0]),
+                device_id_type=MESH,
+            )
+
+        slabs_of = {1: slice(4, 6), -1: slice(0, 2), 0: slice(0, 6)}
+        row_from = {1: slice(23, 25), -1: slice(7, 9), 0: slice(7, 25)}
+        row_to = {1: slice(7, 9), -1: slice(23, 25), 0: slice(7, 25)}
+        for dx in (1, -1, 0):
+            for dy in (1, -1, 0):
+                sx, sy = (1 - dx) // 2, (1 - dy) // 2
+                if dx or dy:
+                    src = part.at[:, slabs_of[dx], row_from[dy]]
+                    if dx and dy:
+                        dst = from_xy.at[sx, sy, :, :, 7:9]
+                    elif dx:
+                        dst = from_x.at[sx, :, :, 7:25]
+                    else:
+                        dst = from_y.at[sy, :, :, 7:9]
+                    copy(((dx, dy, 0), "cells"), src, dst)
+                    copy(
+                        ((dx, dy, 0), "column"),
+                        tile.at[row_from[dy]],
+                        from_plane.at[1 - dx, 1 - dy, row_to[dy]],
+                    )
+                for s, dz in ((0, 1), (1, -1)):
+                    copy(
+                        ((dx, dy, dz), "column"),
+                        tile.at[row_from[dy]],
+                        from_z.at[s, 1 - dx, 1 - dy, row_to[dy]],
+                    )
+        return copies
+
+    parts = part_copies()
+
+    def drag_copies():
+        copies = {}
+        slab_from, slab_to = {1: 4, -1: 1, 0: slice(1, 5)}, {1: 0, -1: 5, 0: slice(1, 5)}
+        row_from = {1: slice(23, 24), -1: slice(8, 9), 0: slice(8, 24)}
+        row_to = {1: slice(7, 8), -1: slice(24, 25), 0: slice(8, 24)}
+        for dx in (1, -1, 0):
+            for dy in (1, -1, 0):
+                if dx or dy:
+                    number = len(copies)
+                    copies[(dx, dy, 0)] = pltpu.make_async_remote_copy(
+                        src_ref=drag.at[slab_from[dx], row_from[dy]],
+                        dst_ref=drag.at[slab_to[dx], row_to[dy]],
+                        send_sem=drag_send.at[number],
+                        recv_sem=drag_recv.at[number],
+                        device_id=device(dx, dy, 0),
+                        device_id_type=MESH,
+                    )
+        return copies
+
+    drags = drag_copies()
 
     def send_x(turn):
         for (dx, dy, dz), copy in exchanges[turn].items():
@@ -215,9 +317,10 @@
         for (dx, dy, dz), copy in exchanges[turn].items():
             pl.when(exists(-dx, -dy, -dz))(copy.wait_recv)
 
-    def column_of(index, x):
-        names = ZPLUS if VELOCITY[index][2] > 0 else ZMINUS
-        return 8 * names.index(index) + 1 + x
+    def column_of(index, x, turn):
+        up = VELOCITY[index][2] > 0
+        k = (ZPLUS if up else ZMINUS).index(index)
+        return 16 * k + 2 * (x + 1) + up if turn == 2 else 8 * k + 1 + x
 
     def gather(turn, x, h):
         values = []
@@ -230,8 +333,10 @@
             value = pads[turn, x + 1 - cx, slot, start : start + 8, :]
             if cz:
                 s = 0 if cz > 0 else 1
-                column = column_of(index, (x - cx) % NX)
-                if 0 <= x - cx < NX:
+                column = column_of(index, x - cx if turn == 2 else (x - cx) % NX, turn)
+                if turn == 2:
+                    halo = zrecv[2, 0, start : start + 8, :]
+                elif 0 <= x - cx < NX:
                     halo = zrecv[turn, s, start : start + 8, :]
                 else:
                     halo = zedge[turn, s, 0 if cx > 0 else 1, 8 * h : 8 * h + 8, :]
@@ -247,12 +352,34 @@
             value = values[index]
             if cz:
                 s = 0 if cz > 0 else 1
-                column = column_of(index, x)
+                column = column_of(index, x, turn)
                 value = pltpu.roll(value, column + 1 if cz > 0 else column, 1)
                 packed[s][h] = jnp.where(lane == column, value, packed[s][h])
             pads[turn, x + 1, SLOT[index], rows, :] = value
             if index == 9:
                 pads[turn, x + 1, TWIN, rows, :] = value
+
+    def scatter_open(x, h, values, packed):
+        rows = slice(ROW + 8 * h, ROW + 8 * h + 8)
+        for k in range(5):
+            column = 16 * k + 2 * (x + 1)
+            both = jnp.where(last, values[ZPLUS[k]], values[ZMINUS[k]])
+            packed[h] = jnp.where(half == column // 2, pltpu.roll(both, column + 1, 1), packed[h])
+        for index in range(19):
+            cz = VELOCITY[index][2]
+            value = values[index]
+            if cz:
+                value = pltpu.roll(value, 1 if cz > 0 else NZ - 1, 1)
+                value = jnp.where(first if cz > 0 else last, 0.0, value)
+            pads[1, x + 1, TWIN if index == 9 else SLOT[index], rows, :] = value
+
+    def pack_drag(x, h, packed):
+        rows = slice(8 * h, 8 * h + 8)
+        value = jnp.where(labels[x, rows, :] == 1, design[x, rows, :], 0.0)
+        drag[x + 1, ROW + 8 * h : ROW + 8 * h + 8, :] = value
+        column = 64 + 2 * (x + 1)
+        for s, shift in ((0, column + 1), (1, column)):
+            packed[s][h] = jnp.where(lane == column, pltpu.roll(value, shift, 1), packed[s][h])
 
     def stage(turn, block):
         zero = jnp.zeros((8, NZ), F32)
@@ -260,12 +387,16 @@
         for x in (0, 3):
             for h in range(HALVES):
                 scatter(turn, x, h, block(x, h), packed)
+                if turn == 0:
+                    pack_drag(x, h, packed)
         if turn == 0:
             pl.semaphore_wait(barrier, len(partners))
         send_x(turn)
         for x in (1, 2):
             for h in range(HALVES):
                 scatter(turn, x, h, block(x, h), packed)
+                if turn == 0:
+                    pack_drag(x, h, packed)
         for s in range(2):
             for h in range(HALVES):
                 zsend[turn, s, 8 * h : 8 * h + 8, :] = packed[s][h]
@@ -388,35 +519,194 @@
 
     stage(0, block_one)
 
+    for offset, copy in drags.items():
+        pl.when(exists(*offset))(copy.start)
+
     receive(0)
-    stage(1, lambda x, h: collide(1, gather(0, x, h), x, h))
-
-    receive(1)
+    zero = jnp.zeros((8, NZ), F32)
+    packed = [zero] * HALVES
+    for x in range(NX):
+        for h in range(HALVES):
+            values = collide(1, gather(0, x, h), x, h)
+            scatter_open(x, h, values, packed)
+    for h in range(HALVES):
+        zpart[ROW + 8 * h : ROW + 8 * h + 8, :] = packed[h]
+
+    def added_up(terms):
+        out = [None] * 4
+        for index, value in terms:
+            for f, c in enumerate((1,) + VELOCITY[index]):
+                if c:
+                    if out[f] is None:
+                        out[f] = value if c > 0 else -value
+                    else:
+                        out[f] = out[f] + value if c > 0 else out[f] - value
+        return [zero if value is None else value for value in out]
+
+    def reaches(h, cy):
+        return 0 <= h < HALVES or (h < 0 and cy < 0) or (h >= HALVES and cy > 0)
+
+    def own_part(x, h):
+        terms = []
+        for index in range(19):
+            cx, cy, _ = VELOCITY[index]
+            if 0 <= x - cx < NX and reaches(h, cy):
+                slot = TWIN if index == 9 else SLOT[index]
+                start = ROW + 8 * h - cy
+                terms.append((index, pads[1, x + 1 - cx, slot, start : start + 8, :]))
+        if len(terms) == 19:
+            return moments([value for _, value in terms])
+        return added_up(terms)
+
+    BLOCKS = range(-1, HALVES + 1)
+    tiles = [zero for _ in BLOCKS]
+
+    def part_slab(x):
+        for h in BLOCKS:
+            rows = slice(ROW + 8 * h, ROW + 8 * h + 8)
+            for f, value in enumerate(own_part(x, h)):
+                part[f, x + 1, rows, :] = value
+                column = 64 + 16 * f + 2 * (x + 1)
+                tiles[h + 1] = jnp.where(
+                    half == column // 2, pltpu.roll(value, column + 1, 1), tiles[h + 1]
+                )
+
+    for x in (-1, 0, 3, 4):
+        part_slab(x)
+    for (offset, kind), copy in parts.items():
+        if kind == "cells" and offset[0]:
+            pl.when(exists(*offset))(copy.start)
+    for x in (1, 2):
+        part_slab(x)
+    for (offset, kind), copy in parts.items():
+        if kind == "cells" and not offset[0]:
+            pl.when(exists(*offset))(copy.start)
+
+    for h in BLOCKS:
+        terms = []
+        for k, index in enumerate(ZPLUS):
+            cx, cy, _ = VELOCITY[index]
+            value = zero
+            if reaches(h, cy):
+                start = ROW + 8 * h - cy
+                value = zpart[start : start + 8, :]
+                shift = (2 * cx - 16 * k) % NZ
+                value = pltpu.roll(value, shift, 1) if shift else value
+            terms.append(value)
+        weight = (terms[0] + (terms[1] + terms[2])) + (terms[3] + terms[4])
+        sums = (weight, terms[1] - terms[2], terms[3] - terms[4], jnp.where(even, weight, -weight))
+        for f, value in enumerate(sums):
+            value = jnp.where(lane < 16, value, 0.0)
+            tiles[h + 1] = tiles[h + 1] + (pltpu.roll(value, 16 * f, 1) if f else value)
+        tile[ROW + 8 * h : ROW + 8 * h + 8, :] = tiles[h + 1]
+    columns = [item for item in parts.items() if item[0][1] == "column"]
+    for (offset, _), copy in sorted(columns, key=lambda item: -sum(map(abs, item[0][0]))):
+        pl.when(exists(*offset))(copy.start)
+
+    for (dx, dy, dz), copy in drags.items():
+        pl.when(exists(-dx, -dy, -dz))(copy.wait_recv)
+    for ((dx, dy, dz), _), copy in parts.items():
+        pl.when(exists(-dx, -dy, -dz))(copy.wait_recv)
+
+    def all_around(read, h, middle=None):
+        rows = slice(ROW + 8 * h, ROW + 8 * h + 8)
+        sums = []
+        for a in range(3):
+            terms = [middle if middle is not None and a == b == 1 else read(a, b, rows) for b in range(3)]
+            sums.append((terms[0] + terms[1]) + terms[2])
+        below, above = pltpu.roll(sums[0], NZ - 8, 1), pltpu.roll(sums[2], 8, 1)
+        return sums[1] + jnp.where(
+            place < 2, below, jnp.where((place == 4) | (place == 5), above, 0.0)
+        )
+
+    through = [[all_around(lambda a, b, r, s=s: from_z[s, a, b, r, :], h) for h in BLOCKS] for s in range(2)]
+    inward = [jnp.where(even, low, pltpu.roll(high, NZ - 2, 1)) for low, high in zip(*through)]
     lost = []
 
-    def block_final(x, h):
-        rows = slice(8 * h, 8 * h + 8)
-        solidity = design[x, rows, :]
-        fluid = labels[x, rows, :] == 1
-        density, jx, jy, jz = moments(gather(1, x, h))
-        inverse = jnp.where(fluid, 1.0 / jnp.where(fluid, density, 1.0), 0.0)
-        v = (jx * inverse, jy * inverse, jz * inverse)
+    def gradient(solidity, seen, density, momentum):
+        inverse = jnp.where(seen, 1.0 / jnp.where(seen, density, 1.0), 0.0)
+        v = [m * inverse for m in momentum]
         square = v[0] * v[0] + v[1] * v[1] + v[2] * v[2]
-        direct = 10.0 * density * square
-        raw[x, rows, :] = direct
-        lost.append(solidity * direct)
-        base = -10.0 * solidity * square
         twice = 20.0 * solidity
-        e = (twice * v[0], twice * v[1], twice * v[2])
-        g = [base] * 19
-        for i in PAIRS:
-            ce = along(i, e)
-            g[i], g[i + 1] = base + ce, base - ce
-        return reverse(g)
-
-    stage(2, block_final)
-
-    receive(2)
+        return square, -10.0 * solidity * square, [twice * a for a in v]
+
+    for x in (0, 1, 2, 3, -1, 4):
+        for h in BLOCKS:
+            rows = slice(ROW + 8 * h, ROW + 8 * h + 8)
+            total = []
+            for f in range(4):
+                value = part[f, x + 1, rows, :]
+                if x < 1:
+                    value = value + from_x[0, f, x + 1, rows, :]
+                if x > 2:
+                    value = value + from_x[1, f, x - 3, rows, :]
+                side = 0 if h < 1 else 1
+                near = slice(8 * (h + 1 - 2 * side), 8 * (h + 1 - 2 * side) + 8)
+                value = value + from_y[side, f, x + 1, near, :]
+                if x < 1:
+                    value = value + from_xy[0, side, f, x + 1, near, :]
+                if x > 2:
+                    value = value + from_xy[1, side, f, x - 3, near, :]
+                column = 16 * f + 2 * (x + 1)
+                turned = pltpu.roll(inward[h + 1], NZ - column, 1) if column else inward[h + 1]
+                value = value + jnp.where(ends, turned, 0.0)
+                total.append(value)
+            if 0 <= x < NX and 0 <= h < HALVES:
+                own = slice(8 * h, 8 * h + 8)
+                solidity, seen = design[x, own, :], labels[x, own, :] == 1
+            else:
+                solidity = drag[x + 1, rows, :]
+                seen = solidity > 0.0
+            square, base, e = gradient(solidity, seen, total[0], total[1:])
+            if 0 <= x < NX and 0 <= h < HALVES:
+                direct = 10.0 * total[0] * square
+                raw[x, own, :] = direct
+                lost.append(solidity * direct)
+            for index in range(19):
+                cx, cy, cz = VELOCITY[index]
+                if not (0 <= x + cx < NX and (0 <= h < HALVES or (cy > 0 if h < 0 else cy < 0))):
+                    continue
+                value = base
+                for c, a in zip((cx, cy, cz), e):
+                    if c:
+                        value = value - a if c > 0 else value + a
+                if cz:
+                    value = pltpu.roll(value, column_of(index, x, 2) + (cz > 0), 1)
+                pads[2, x + 1, SLOT[index], rows, :] = value
+                if index == 9:
+                    pads[2, x + 1, TWIN, rows, :] = value
+
+    for h in BLOCKS:
+        rows = slice(ROW + 8 * h, ROW + 8 * h + 8)
+        about = all_around(lambda a, b, r: from_plane[a, b, r, :], h, tile[rows, :])
+        about = about + jnp.where(
+            even,
+            pltpu.roll(through[1][h + 1], NZ - 65, 1),
+            pltpu.roll(through[0][h + 1], NZ - 63, 1),
+        )
+        total = [about] + [pltpu.roll(about, NZ - 16 * f, 1) for f in range(1, 4)]
+
+        def drags_at(low, high, column):
+            return jnp.where(
+                even, pltpu.roll(high, NZ - column, 1), pltpu.roll(low, NZ + 1 - column, 1)
+            )
+
+        solidity = drags_at(zrecv[0, 0, rows, :], zrecv[0, 1, rows, :], 64)
+        if 0 <= h < HALVES:
+            own = slice(8 * h, 8 * h + 8)
+            below = drags_at(zedge[0, 0, 0, own, :], zedge[0, 1, 0, own, :], 72)
+            above = drags_at(zedge[0, 0, 1, own, :], zedge[0, 1, 1, own, :], 56)
+            solidity = jnp.where(place == 0, below, jnp.where(place == 5, above, solidity))
+        _, base, e = gradient(solidity, solidity > 0.0, total[0], total[1:])
+        base = base + jnp.where(even, e[2], -e[2])
+        out = None
+        for k, index in enumerate(ZPLUS):
+            value = base
+            for c, a in zip(VELOCITY[index][:2], e):
+                if c:
+                    value = value - a if c > 0 else value + a
+            out = value if k == 0 else jnp.where(lane >= 16 * k, pltpu.roll(value, 16 * k, 1), out)
+        zrecv[2, 0, rows, :] = out
 
     def block_two(x, h):
         rows = slice(8 * h, 8 * h + 8)
@@ -483,11 +773,15 @@
                 adj[x, i, rows, :] = back[i]
         stores.append(pltpu.make_async_copy(adj.at[x], adj_hbm.at[:, x], store_sem.at[x]))
         stores[-1].start()
-    for turn in range(ROUNDS):
+    for turn in exchanges:
         for (dx, dy, dz), copy in exchanges[turn].items():
             pl.when(exists(dx, dy, dz))(copy.wait_send)
+    for offset, copy in drags.items():
+        pl.when(exists(*offset))(copy.wait_send)
+    for (offset, _), copy in parts.items():
+        pl.when(exists(*offset))(copy.wait_send)
     mine = added(red_p, sent)
-    last_sent = spread(red_y, gy, column, len(plane))
+    last_sent = spread(red_y, gy, line, len(plane))
     mine = added(red_y, last_sent)
     sent = sent + last_sent
 
@@ -567,12 +861,25 @@
                 pltpu.VMEM((ROUNDS, 2, 2, NY, NZ), F32),
                 pltpu.VMEM((2, 5) + cells, F32),
                 pltpu.VMEM(cells, F32),
+                pltpu.VMEM((4, NX + 2, NY + 16, NZ), F32),
+                pltpu.VMEM((NY + 16, NZ), F32),
+                pltpu.VMEM((NY + 16, NZ), F32),
+                pltpu.VMEM((2, 4, 2, NY + 16, NZ), F32),
+                pltpu.VMEM((2, 4, NX + 2, 16, NZ), F32),
+                pltpu.VMEM((2, 2, 4, 2, 16, NZ), F32),
+                pltpu.VMEM((3, 3, NY + 16, NZ), F32),
+                pltpu.VMEM((2, 3, 3, NY + 16, NZ), F32),
+                pltpu.VMEM((NX + 2, NY + 16, NZ), F32),
                 pltpu.VMEM((nx * nz, 8, NZ), F32),
                 pltpu.VMEM((ny, 8, NZ), F32),
                 pltpu.SemaphoreType.DMA((6,)),
                 pltpu.SemaphoreType.DMA((NX + 1,)),
                 pltpu.SemaphoreType.DMA((ROUNDS, 18)),
                 pltpu.SemaphoreType.DMA((ROUNDS, 18)),
+                pltpu.SemaphoreType.DMA((34,)),
+                pltpu.SemaphoreType.DMA((34,)),
+                pltpu.SemaphoreType.DMA((8,)),
+                pltpu.SemaphoreType.DMA((8,)),
                 pltpu.SemaphoreType.DMA((partners,)),
                 pltpu.SemaphoreType.DMA((partners,)),
             ],

time: 42.1 us -> 41 us (0.974)
  Pallas kernels: 41.3 us -> 40.2 us
    pallas_call x1, Pallas kernels: 38.9 us -> 37.8 us  [body(): pl.pallas_call(lambda *refs: kernel((nx, ny, nz), *refs), out_shape=(jax....]
where the time goes in v4:
time: 41 us; the launch traced here: 40.9 us
  Pallas kernels  40.2 us (98%)
  between operations  0.64 us (2%)
    pallas_call x1, Pallas kernels, body(): pl.pallas_call(lambda *refs: kernel((nx, ny, nz), *refs), out_shape=(jax....  37.8 us
    pallas_call x1, Pallas kernels, body(): pl.pallas_call(finish, out_shape=(jax.ShapeDtypeStruct((19,) + cells, F32...  2.42 us

profile of v4, /device:TPU:1, one launch (start us, length us, event | category | flops | bytes accessed | tf_op | source)
XLA Modules:
  0.0 40.9 jit_solution(13365320201172171400)
XLA Ops:
  0.6 37.8 %shard_map.58 = (f32[19,4,16,128]{3,2,1,0:T(8,128)}, f32[4,16,128]{2,1,0:T(8,128)}, f32[2]{0:T(128)}) custom-call(f32[19,4,16,128]{3,2,1,0:T(8,128)} %refs_0_.1, f32[4,16,128]{2,1,0:T(8,128)} %refs_1_.1, s32[4,16,128]{2,1,0:T(8,128)} %refs_2_.1), custom_call_target="tpu_custom_call" | custom-call | flops 10000000 | bytes 1500000 | tf_op jit(solution)/shard_map/pallas_call | solution.py:840
  38.4 2.4 %shard_map.59 = (f32[19,4,16,128]{3,2,1,0:T(8,128)}, f32[4,16,128]{2,1,0:T(8,128)}, f32[1]{0:T(128)}) custom-call(f32[2]{0:T(128)} %get-tuple-element.9.sums_in, f32[19,4,16,128]{3,2,1,0:T(8,128)} %get-tuple-element.10.adj_in, f32[4,16,128]{2,1,0:T(8,128)} %get-tuple-element.11.raw_in), custom_call_target="tpu_custom_call" | custom-call | tf_op jit(solution)/shard_map/pallas_call | solution.py:893

commit v5 on v4

--- a/solution.py
+++ b/solution.py
@@ -729,21 +729,22 @@
     lost_of = lost[0]
     for term in lost[1:]:
         lost_of = lost_of + term
-    row = lax.broadcasted_iota(jnp.int32, (8, NZ), 0)
-    mine = jnp.where(
-        row == 0,
-        jnp.sum(lost_of, axis=0, keepdims=True),
-        jnp.where(row == 1, jnp.sum(sizes_of, axis=0, keepdims=True), 0.0),
-    )
+    left = lax.broadcasted_iota(jnp.int32, (1, NZ), 1) < NZ // 2
+
+    def folded(value):
+        value = value + pltpu.roll(value, NZ // 2, 1)
+        return jnp.sum(value, axis=0, keepdims=True)
+
+    mine = jnp.where(left, folded(lost_of), folded(sizes_of))
 
     def spread(buffer, me, steps, base):
-        buffer[me] = mine
+        buffer[pl.ds(me, 1), :] = mine
         copies = []
         for number, step in enumerate(steps):
             copies.append(
                 pltpu.make_async_remote_copy(
-                    src_ref=buffer.at[me],
-                    dst_ref=buffer.at[me],
+                    src_ref=buffer.at[pl.ds(me, 1)],
+                    dst_ref=buffer.at[pl.ds(me, 1)],
                     send_sem=red_send.at[base + number],
                     recv_sem=red_recv.at[base + number],
                     device_id=device(*step),
@@ -757,10 +758,7 @@
     def added(buffer, copies):
         for copy in copies:
             copy.wait_recv()
-        terms = [buffer[k] for k in range(len(copies) + 1)]
-        while len(terms) > 1:
-            terms = [a + b for a, b in zip(terms[::2], terms[1::2])]
-        return terms[0]
+        return jnp.sum(buffer[...], axis=0, keepdims=True)
 
     sent = spread(red_p, gx * nz + gz, plane, 0)
     stores = [pltpu.make_async_copy(raw, raw_hbm, store_sem.at[NX])]
@@ -786,8 +784,8 @@
     sent = sent + last_sent
 
     cells = NX * NY * NZ * nx * ny * nz
-    loss = jnp.sum(jnp.where(row == 0, mine, 0.0))
-    size = jnp.sum(jnp.where(row == 1, mine, 0.0))
+    loss = jnp.sum(jnp.where(left, mine, 0.0))
+    size = jnp.sum(jnp.where(left, 0.0, mine))
     sums_ref[0] = 20.0 * loss / cells
     sums_ref[1] = size / cells + 1e-06
 
@@ -870,8 +868,8 @@
                 pltpu.VMEM((3, 3, NY + 16, NZ), F32),
                 pltpu.VMEM((2, 3, 3, NY + 16, NZ), F32),
                 pltpu.VMEM((NX + 2, NY + 16, NZ), F32),
-                pltpu.VMEM((nx * nz, 8, NZ), F32),
-                pltpu.VMEM((ny, 8, NZ), F32),
+                pltpu.VMEM((nx * nz, NZ), F32),
+                pltpu.VMEM((ny, NZ), F32),
                 pltpu.SemaphoreType.DMA((6,)),
                 pltpu.SemaphoreType.DMA((NX + 1,)),
                 pltpu.SemaphoreType.DMA((ROUNDS, 18)),

time: 41 us -> 40.1 us (0.978)
  Pallas kernels: 40.2 us -> 39.4 us
    pallas_call x1, Pallas kernels: 37.8 us -> 36.9 us  [body(): pl.pallas_call(lambda *refs: kernel((nx, ny, nz), *refs), out_shape=(jax....]
where the time goes in v5:
time: 40.1 us; the launch traced here: 40 us
  Pallas kernels  39.4 us (98%)
  between operations  0.64 us (2%)
    pallas_call x1, Pallas kernels, body(): pl.pallas_call(lambda *refs: kernel((nx, ny, nz), *refs), out_shape=(jax....  36.9 us
    pallas_call x1, Pallas kernels, body(): pl.pallas_call(finish, out_shape=(jax.ShapeDtypeStruct((19,) + cells, F32...  2.42 us

profile of v5, /device:TPU:1, one launch (start us, length us, event | category | flops | bytes accessed | tf_op | source)
XLA Modules:
  0.0 40.0 jit_solution(6143898158597787721)
XLA Ops:
  0.6 36.9 %shard_map.58 = (f32[19,4,16,128]{3,2,1,0:T(8,128)}, f32[4,16,128]{2,1,0:T(8,128)}, f32[2]{0:T(128)}) custom-call(f32[19,4,16,128]{3,2,1,0:T(8,128)} %refs_0_.1, f32[4,16,128]{2,1,0:T(8,128)} %refs_1_.1, s32[4,16,128]{2,1,0:T(8,128)} %refs_2_.1), custom_call_target="tpu_custom_call" | custom-call | flops 10000000 | bytes 1500000 | tf_op jit(solution)/shard_map/pallas_call | solution.py:838
  37.6 2.4 %shard_map.59 = (f32[19,4,16,128]{3,2,1,0:T(8,128)}, f32[4,16,128]{2,1,0:T(8,128)}, f32[1]{0:T(128)}) custom-call(f32[2]{0:T(128)} %get-tuple-element.9.sums_in, f32[19,4,16,128]{3,2,1,0:T(8,128)} %get-tuple-element.10.adj_in, f32[4,16,128]{2,1,0:T(8,128)} %get-tuple-element.11.raw_in), custom_call_target="tpu_custom_call" | custom-call | tf_op jit(solution)/shard_map/pallas_call | solution.py:891

commit v6 on v5

--- a/solution.py
+++ b/solution.py
@@ -182,12 +182,24 @@
         from_x[1] = jnp.zeros((4, 2, NY + 16, NZ), F32)
 
     barrier = pltpu.get_barrier_semaphore()
-    plane = [(a, 0, b) for a in range(nx) for b in range(nz) if a or b]
-    line = [(0, k, 0) for k in range(1, ny)]
+    core = lax.rem(gz, 2)
+    twin = gz + 1 - 2 * core
+
+    def far(step):
+        return -sum(min(a, n - a) for a, n in zip(step, sizes))
+
+    line = sorted([(0, k, 0) for k in range(1, ny)], key=far)
+    plane = [(a, 0, b) for a in range(nx) for b in range(0, nz, 2) if a or b]
+    plane = sorted(plane, key=far)
+    pairs = [device(*step) for step in line]
+    pairs = [there for step in pairs for there in (step, {**step, "gz": twin})]
+    pairs.append({"gx": gx, "gy": gy, "gz": twin})
     corners = [(a, b, c) for a in (1, -1) for b in (1, -1) for c in (1, -1)]
-    partners = [n for n in NEIGHBOURS if n[1] and (n[0] or n[2])] + corners + plane + line
+    faces = [(1, 0, 0), (-1, 0, 0), (0, 1, 0), (0, -1, 0)]
+    around = [n for n in NEIGHBOURS if n not in faces] + corners + plane
+    partners = [device(*n) for n in around] + pairs
     for partner in partners:
-        pl.semaphore_signal(barrier, inc=1, device_id=device(*partner), device_id_type=MESH)
+        pl.semaphore_signal(barrier, inc=1, device_id=partner, device_id_type=MESH)
 
     lane = lax.broadcasted_iota(jnp.int32, (8, NZ), 1)
     half = lane // 2
@@ -304,13 +316,15 @@
     drags = drag_copies()
 
     def send_x(turn):
-        for (dx, dy, dz), copy in exchanges[turn].items():
+        for (dx, dy, dz), copy in sorted(exchanges[turn].items(), key=lambda item: not item[0][1]):
             if dx and not dz:
                 pl.when(exists(dx, dy, dz))(copy.start)
 
     def send_rest(turn):
         rest = [item for item in exchanges[turn].items() if item[0][2] or not item[0][0]]
-        for (dx, dy, dz), copy in sorted(rest, key=lambda item: not item[0][1]):
+        for (dx, dy, dz), copy in sorted(
+            rest, key=lambda item: (not item[0][1], -sum(map(abs, item[0])))
+        ):
             pl.when(exists(dx, dy, dz))(copy.start)
 
     def receive(turn):
@@ -737,17 +751,17 @@
 
     mine = jnp.where(left, folded(lost_of), folded(sizes_of))
 
-    def spread(buffer, me, steps, base):
+    def spread(buffer, me, targets, base):
         buffer[pl.ds(me, 1), :] = mine
         copies = []
-        for number, step in enumerate(steps):
+        for number, target in enumerate(targets):
             copies.append(
                 pltpu.make_async_remote_copy(
                     src_ref=buffer.at[pl.ds(me, 1)],
                     dst_ref=buffer.at[pl.ds(me, 1)],
                     send_sem=red_send.at[base + number],
                     recv_sem=red_recv.at[base + number],
-                    device_id=device(*step),
+                    device_id=target,
                     device_id_type=MESH,
                 )
             )
@@ -760,7 +774,7 @@
             copy.wait_recv()
         return jnp.sum(buffer[...], axis=0, keepdims=True)
 
-    sent = spread(red_p, gx * nz + gz, plane, 0)
+    sent = spread(red_y, gy * 2 + core, pairs, 0)
     stores = [pltpu.make_async_copy(raw, raw_hbm, store_sem.at[NX])]
     stores[0].start()
     for x in range(NX):
@@ -778,9 +792,9 @@
         pl.when(exists(*offset))(copy.wait_send)
     for (offset, _), copy in parts.items():
         pl.when(exists(*offset))(copy.wait_send)
-    mine = added(red_p, sent)
-    last_sent = spread(red_y, gy, line, len(plane))
-    mine = added(red_y, last_sent)
+    mine = added(red_y, sent)
+    last_sent = spread(red_p, gx * (nz // 2) + gz // 2, [device(*step) for step in plane], len(pairs))
+    mine = added(red_p, last_sent)
     sent = sent + last_sent
 
     cells = NX * NY * NZ * nx * ny * nz
@@ -831,7 +845,7 @@
 
 def solution(mesh):
     nx, ny, nz = (mesh.shape[a] for a in ("gx", "gy", "gz"))
-    partners = nx * nz + ny - 2
+    partners = nx * nz // 2 + 2 * ny - 2
 
     def body(populations, design, labels):
         cells = (NX, NY, NZ)
@@ -868,8 +882,8 @@
                 pltpu.VMEM((3, 3, NY + 16, NZ), F32),
                 pltpu.VMEM((2, 3, 3, NY + 16, NZ), F32),
                 pltpu.VMEM((NX + 2, NY + 16, NZ), F32),
-                pltpu.VMEM((nx * nz, NZ), F32),
-                pltpu.VMEM((ny, NZ), F32),
+                pltpu.VMEM((nx * nz // 2, NZ), F32),
+                pltpu.VMEM((2 * ny, NZ), F32),
                 pltpu.SemaphoreType.DMA((6,)),
                 pltpu.SemaphoreType.DMA((NX + 1,)),
                 pltpu.SemaphoreType.DMA((ROUNDS, 18)),

time: 40.1 us -> 39.7 us (0.990)
  Pallas kernels: 39.4 us -> 38.9 us
    pallas_call x1, Pallas kernels: 36.9 us -> 36.5 us  [body(): pl.pallas_call(lambda *refs: kernel((nx, ny, nz), *refs), out_shape=(jax....]
where the time goes in v6:
time: 39.7 us; the launch traced here: 39.6 us
  Pallas kernels  38.9 us (98%)
  between operations  0.64 us (2%)
    pallas_call x1, Pallas kernels, body(): pl.pallas_call(lambda *refs: kernel((nx, ny, nz), *refs), out_shape=(jax....  36.5 us
    pallas_call x1, Pallas kernels, body(): pl.pallas_call(finish, out_shape=(jax.ShapeDtypeStruct((19,) + cells, F32...  2.42 us

profile of v6, /device:TPU:1, one launch (start us, length us, event | category | flops | bytes accessed | tf_op | source)
XLA Modules:
  0.0 39.6 jit_solution(3431716060446357196)
XLA Ops:
  0.6 36.5 %shard_map.58 = (f32[19,4,16,128]{3,2,1,0:T(8,128)}, f32[4,16,128]{2,1,0:T(8,128)}, f32[2]{0:T(128)}) custom-call(f32[19,4,16,128]{3,2,1,0:T(8,128)} %refs_0_.1, f32[4,16,128]{2,1,0:T(8,128)} %refs_1_.1, s32[4,16,128]{2,1,0:T(8,128)} %refs_2_.1), custom_call_target="tpu_custom_call" | custom-call | flops 10000000 | bytes 1500000 | tf_op jit(solution)/shard_map/pallas_call | solution.py:852
  37.1 2.4 %shard_map.59 = (f32[19,4,16,128]{3,2,1,0:T(8,128)}, f32[4,16,128]{2,1,0:T(8,128)}, f32[1]{0:T(128)}) custom-call(f32[2]{0:T(128)} %get-tuple-element.9.sums_in, f32[19,4,16,128]{3,2,1,0:T(8,128)} %get-tuple-element.10.adj_in, f32[4,16,128]{2,1,0:T(8,128)} %get-tuple-element.11.raw_in), custom_call_target="tpu_custom_call" | custom-call | tf_op jit(solution)/shard_map/pallas_call | solution.py:905

commit v7 on v6

--- a/solution.py
+++ b/solution.py
@@ -794,8 +794,11 @@
         pl.when(exists(*offset))(copy.wait_send)
     mine = added(red_y, sent)
     last_sent = spread(red_p, gx * (nz // 2) + gz // 2, [device(*step) for step in plane], len(pairs))
+    for copy in stores:
+        copy.wait()
+    for copy in sent:
+        copy.wait_send()
     mine = added(red_p, last_sent)
-    sent = sent + last_sent
 
     cells = NX * NY * NZ * nx * ny * nz
     loss = jnp.sum(jnp.where(left, mine, 0.0))
@@ -803,10 +806,8 @@
     sums_ref[0] = 20.0 * loss / cells
     sums_ref[1] = size / cells + 1e-06
 
-    for copy in sent:
+    for copy in last_sent:
         copy.wait_send()
-    for copy in stores:
-        copy.wait()
 
 
 def finish(sums_in, adj_in, raw_in, adj_out, sens_out, obj_out, raw, adj, sums, sem):

time: 39.7 us -> 39.7 us (level)
  no operation moved by 1% of the time
where the time goes in v7:
time: 39.7 us; the launch traced here: 39.5 us
  Pallas kernels  38.9 us (98%)
  between operations  0.64 us (2%)
    pallas_call x1, Pallas kernels, body(): pl.pallas_call(lambda *refs: kernel((nx, ny, nz), *refs), out_shape=(jax....  36.5 us
    pallas_call x1, Pallas kernels, body(): pl.pallas_call(finish, out_shape=(jax.ShapeDtypeStruct((19,) + cells, F32...  2.42 us

profile of v7, /device:TPU:1, one launch (start us, length us, event | category | flops | bytes accessed | tf_op | source)
XLA Modules:
  0.0 39.5 jit_solution(5886342884059119975)
XLA Ops:
  0.6 36.5 %shard_map.58 = (f32[19,4,16,128]{3,2,1,0:T(8,128)}, f32[4,16,128]{2,1,0:T(8,128)}, f32[2]{0:T(128)}) custom-call(f32[19,4,16,128]{3,2,1,0:T(8,128)} %refs_0_.1, f32[4,16,128]{2,1,0:T(8,128)} %refs_1_.1, s32[4,16,128]{2,1,0:T(8,128)} %refs_2_.1), custom_call_target="tpu_custom_call" | custom-call | flops 10000000 | bytes 1500000 | tf_op jit(solution)/shard_map/pallas_call | solution.py:853
  37.1 2.4 %shard_map.59 = (f32[19,4,16,128]{3,2,1,0:T(8,128)}, f32[4,16,128]{2,1,0:T(8,128)}, f32[1]{0:T(128)}) custom-call(f32[2]{0:T(128)} %get-tuple-element.9.sums_in, f32[19,4,16,128]{3,2,1,0:T(8,128)} %get-tuple-element.10.adj_in, f32[4,16,128]{2,1,0:T(8,128)} %get-tuple-element.11.raw_in), custom_call_target="tpu_custom_call" | custom-call | tf_op jit(solution)/shard_map/pallas_call | solution.py:906
